TPU v7x, 128 devices: a whole 4x4x4 slice. The times are simulated.
128 devices in a mesh: dp: 4 (over y_hi, core), grp: 32 (over z, y_lo, x).
Axes of the slice: x: 4, y: 4 (y_hi: 2, y_lo: 2; y = y_hi * 2 + y_lo), z: 4, core: 2. Of those that a mesh axis runs over, the one named last changes fastest.
Arguments:
- token_ids: int32 [4, 4, 8, 4], P('dp'), may hold values from 0 to 128255
- start_pos: int32 [4, 4, 8], P('dp'), may hold values from 0 to 8191
- cache_len: int32 [4, 4, 8], P('dp'), may hold values from 1 to 1020, as said below
- embed_table: bfloat16 [128256, 4096], P(('dp', 'grp')), may hold values from -6 to 6
- norm_gain: float32 [2, 4096], replicated, may hold values from 0.1 to 1.9
- query_key_value_weight: bfloat16 [2, 4096, 6144], P(None, 'grp'), may hold values from -0.09375 to 0.09375
- output_weight: bfloat16 [2, 4096, 4096], P(None, 'grp'), may hold values from -0.09375 to 0.09375
- key_value_cache: bfloat16 [2, 32, 32, 1024, 256], P(None, 'dp', 'grp'), may hold values from -24 to 24, as said below
Outputs:
- decoded: bfloat16 [32, 32, 4, 512], P('dp', 'grp')
Inputs may be any that keep to these rules, and one draw needn't show every extreme that they name: `cache_len`: in every draw some sequence has exactly 1020 live positions and some sequence has exactly 1. `key_value_cache`: keys are stored already rotated.
All inputs are finite; a program needn't handle non-finite values.
Results may differ from a plain program's by a relative error of at most 0.029.
Values may be sent and summed in bfloat16 or wider, within the bound.
A program may use at most 192 MiB of HBM per device.

v0:
```python
import jax
import jax.numpy as jnp
from jax import lax
from jax.sharding import PartitionSpec as P

MODEL_WIDTH = 4096
QUERY_HEADS = 32
KEY_VALUE_HEADS = 8
HEAD_SIZE = 128
DECODER_LAYERS = 2
DECODE_STEPS = 4
REPLICA_ROWS = 8


ROPE_BASE = 500000.0
EPSILON = 1e-05


def swapped(block, axis, bit):
    count = lax.axis_size(axis)
    route = []
    for low in range(count):
        high = low | 1 << bit
        if high != low and high < count:
            route += [(low, high), (high, low)]
    return lax.ppermute(block, axis, route)


def rotate(vectors, position):
    half_width = vectors.shape[-1] // 2
    exponent = jnp.arange(half_width, dtype=jnp.float32) * (2.0 / vectors.shape[-1])
    frequency = jnp.power(jnp.float32(ROPE_BASE), -exponent)
    angles = position.astype(jnp.float32)[..., None] * frequency
    cosine = jnp.cos(angles)
    sine = jnp.sin(angles)
    first_half = vectors[..., :half_width]
    second_half = vectors[..., half_width:]
    return jnp.concatenate(
        [first_half * cosine - second_half * sine, second_half * cosine + first_half * sine],
        axis=-1,
    )


def rms_normed(stream, gain):
    factor = lax.rsqrt(jnp.mean(stream * stream, axis=-1, keepdims=True) + EPSILON)
    return (stream * factor * gain).astype(jnp.bfloat16)


def attend_whole(query_rows, cache_keys, cache_values, keys_new, values_new, lengths, step_no):
    scale = query_rows.shape[-1] ** (-0.5)
    cache_scores = (
        jnp.einsum("rgd,rjd->rgj", query_rows, cache_keys, preferred_element_type=jnp.float32)
        * scale
    )
    fresh_scores = (
        jnp.einsum("rgd,rjd->rgj", query_rows, keys_new, preferred_element_type=jnp.float32) * scale
    )
    cache_mask = (jnp.arange(cache_keys.shape[1], dtype=jnp.int32)[None, :] < lengths[:, None])[
        :, None, :
    ]
    fresh_mask = (jnp.arange(keys_new.shape[1], dtype=jnp.int32) <= step_no)[None, None, :]
    cache_exp = jnp.where(cache_mask, jnp.exp(cache_scores), 0.0)
    fresh_exp = jnp.where(fresh_mask, jnp.exp(fresh_scores), 0.0)
    denominator = jnp.sum(cache_exp, axis=-1, keepdims=True) + jnp.sum(
        fresh_exp, axis=-1, keepdims=True
    )
    cache_weights = (cache_exp / denominator).astype(jnp.bfloat16)
    fresh_weights = (fresh_exp / denominator).astype(jnp.bfloat16)
    attended = jnp.einsum(
        "rgj,rjd->rgd", cache_weights, cache_values, preferred_element_type=jnp.float32
    )
    return attended + jnp.einsum(
        "rgj,rjd->rgd", fresh_weights, values_new, preferred_element_type=jnp.float32
    )


def body(
    token_ids,
    start_pos,
    cache_len,
    embed_table,
    norm_gain,
    query_key_value_weight,
    output_weight,
    key_value_cache,
):
    prompt_group_size = lax.axis_size("grp")
    replica_list = prompt_group_size // KEY_VALUE_HEADS
    prompt_group_index = lax.axis_index("grp")
    replica_number = prompt_group_index // KEY_VALUE_HEADS
    tensor_slice_number = prompt_group_index % KEY_VALUE_HEADS
    heads_per_group = QUERY_HEADS // KEY_VALUE_HEADS
    portion_width = heads_per_group * HEAD_SIZE
    present_layers = query_key_value_weight.shape[0]
    local_row_count = query_key_value_weight.shape[1]
    all_ids = lax.all_gather(token_ids, "dp", axis=0, tiled=True).reshape(-1)
    shard_rows = embed_table.shape[0]
    local_ids = all_ids - lax.axis_index(("dp", "grp")) * shard_rows
    inside = (local_ids >= 0) & (local_ids < shard_rows)
    picked = jnp.take(embed_table, jnp.clip(local_ids, 0, shard_rows - 1), axis=0)
    partial_rows = jnp.where(inside[:, None], picked.astype(jnp.float32), 0.0)
    joined = lax.psum_scatter(partial_rows, ("dp", "grp"), scatter_dimension=0, tiled=True).astype(
        jnp.bfloat16
    )
    for bit_position in range(KEY_VALUE_HEADS.bit_length() - 1):
        partner = swapped(joined, "grp", bit_position)
        upper_bit = prompt_group_index >> bit_position & 1
        joined = jnp.where(
            upper_bit == 0,
            jnp.concatenate([joined, partner], 0),
            jnp.concatenate([partner, joined], 0),
        )
    embedded = joined.reshape(REPLICA_ROWS, DECODE_STEPS, MODEL_WIDTH).astype(jnp.float32)
    query_portion = query_key_value_weight[:, :, : QUERY_HEADS * HEAD_SIZE].reshape(
        present_layers, local_row_count, KEY_VALUE_HEADS, portion_width
    )
    key_portion = query_key_value_weight[
        :, :, QUERY_HEADS * HEAD_SIZE : QUERY_HEADS * HEAD_SIZE + KEY_VALUE_HEADS * HEAD_SIZE
    ].reshape(present_layers, local_row_count, KEY_VALUE_HEADS, HEAD_SIZE)
    value_portion = query_key_value_weight[
        :, :, QUERY_HEADS * HEAD_SIZE + KEY_VALUE_HEADS * HEAD_SIZE :
    ].reshape(present_layers, local_row_count, KEY_VALUE_HEADS, HEAD_SIZE)
    sliced_qkv = jnp.concatenate([query_portion, key_portion, value_portion], axis=-1)
    output_slice_weight = output_weight.reshape(
        present_layers, local_row_count, KEY_VALUE_HEADS, portion_width
    )

    def copied(pieces):
        target = (present_layers, local_row_count, replica_list) + pieces.shape[2:]
        return jnp.broadcast_to(pieces[:, :, None], target).reshape(
            present_layers, local_row_count, -1
        )

    own_qkv, own_out = (
        lax.all_to_all(copied(sliced_qkv), "grp", split_axis=2, concat_axis=1, tiled=True),
        lax.all_to_all(copied(output_slice_weight), "grp", split_axis=2, concat_axis=1, tiled=True),
    )
    lengths = lax.dynamic_index_in_dim(cache_len[0], replica_number, 0, keepdims=False)
    starts = lax.dynamic_index_in_dim(start_pos[0], replica_number, 0, keepdims=False)
    fresh_keys = [
        jnp.zeros((REPLICA_ROWS, DECODE_STEPS, HEAD_SIZE), jnp.bfloat16)
        for layer_no in range(DECODER_LAYERS)
    ]
    fresh_values = [
        jnp.zeros((REPLICA_ROWS, DECODE_STEPS, HEAD_SIZE), jnp.bfloat16)
        for layer_no in range(DECODER_LAYERS)
    ]
    feature_span_block = MODEL_WIDTH // KEY_VALUE_HEADS
    outputs = []
    for step_no in range(DECODE_STEPS):
        stream = embedded[:, step_no]
        positions = starts + step_no
        for layer_no in range(DECODER_LAYERS):
            normed = rms_normed(stream, norm_gain[layer_no])
            projected_output = jnp.dot(
                normed, own_qkv[layer_no], preferred_element_type=jnp.float32
            )
            query_rows = rotate(
                projected_output[:, :portion_width].reshape(
                    REPLICA_ROWS, heads_per_group, HEAD_SIZE
                ),
                positions[:, None],
            ).astype(jnp.bfloat16)
            current_keys = rotate(
                projected_output[:, portion_width : portion_width + HEAD_SIZE], positions
            ).astype(jnp.bfloat16)
            current_values = projected_output[:, portion_width + HEAD_SIZE :].astype(jnp.bfloat16)
            fresh_keys[layer_no] = fresh_keys[layer_no].at[:, step_no].set(current_keys)
            fresh_values[layer_no] = fresh_values[layer_no].at[:, step_no].set(current_values)
            cache_keys = key_value_cache[layer_no, :, 0, :, :HEAD_SIZE]
            cache_values = key_value_cache[layer_no, :, 0, :, HEAD_SIZE:]
            attended = attend_whole(
                query_rows,
                cache_keys,
                cache_values,
                fresh_keys[layer_no],
                fresh_values[layer_no],
                lengths,
                step_no,
            )
            attended = attended.astype(jnp.bfloat16).reshape(REPLICA_ROWS, portion_width)
            partial_value = lax.dot_general(
                attended,
                own_out[layer_no],
                (((1,), (1,)), ((), ())),
                preferred_element_type=jnp.float32,
            )
            summed = partial_value
            for bit_position in range(KEY_VALUE_HEADS.bit_length() - 1):
                summed = summed + swapped(summed, "grp", bit_position)
            stream = stream + summed
        outputs.append(
            lax.dynamic_slice_in_dim(
                stream.astype(jnp.bfloat16),
                tensor_slice_number * feature_span_block,
                feature_span_block,
                1,
            )
        )
    return jnp.stack(outputs, axis=1).reshape(REPLICA_ROWS, 1, DECODE_STEPS, feature_span_block)


def solution(mesh):
    return jax.shard_map(
        body,
        mesh=mesh,
        in_specs=(
            P("dp", None, None, None),
            P("dp", None, None),
            P("dp", None, None),
            P(("dp", "grp"), None),
            P(),
            P(None, "grp", None),
            P(None, "grp", None),
            P(None, "dp", "grp", None, None),
        ),
        out_specs=P("dp", "grp", None, None),
        check_vma=False,
    )
```

profile of v0, /device:TPU:8, one launch (start us, length us, event | category | flops | bytes accessed | tf_op | source)
XLA Modules:
  0.0 647.9 jit_solution(13676873710412291500)
XLA Ops:
  0.0 4.7 copy.199
  4.7 5.6 broadcast_in_dim.132
  10.4 9.4 %all-to-all-start.1 = ((bf16[2,128,16384]{1,0,2:T(2,128)(2,1)}), bf16[2,128,16384]{1,0,2:T(2,128)(2,1)}, u32[]{:S(2)}, u32[]{:S(2)}) async-start(bf16[2,128,16384]{1,0,2:T(2,128)(2,1)} %bitcast.380), calls=%async_computation.1 | async-start | bytes 16777216 | tf_op jit(solution)/shard_map/all_to_all | solution.py:136
  19.8 1.9 copy-done.8
  23.5 4.3 copy.143
  27.8 110.9 %all-to-all-done.1 = bf16[2,128,16384]{1,0,2:T(2,128)(2,1)} async-done(((bf16[2,128,16384]{1,0,2:T(2,128)(2,1)}), bf16[2,128,16384]{1,0,2:T(2,128)(2,1)}, u32[]{:S(2)}, u32[]{:S(2)}) %all-to-all-start.1) | async-done | bytes 8388640 | tf_op jit(solution)/shard_map/all_to_all | solution.py:136
  138.7 9.1 %broadcast_in_dim.127 = bf16[2,128,4,8,768]{1,0,4,3,2:T(2,128)(2,1)} broadcast(bf16[2,128,8,768]{1,0,3,2:T(2,128)(2,1)} %copy.143), dimensions={0,1,3,4} | broadcast | bytes 15728640 | tf_op jit(solution)/shard_map/broadcast_in_dim | solution.py:130
  147.9 10.4 %all-to-all-start = ((bf16[2,128,24576]{1,0,2:T(2,128)(2,1)}), bf16[2,128,24576]{1,0,2:T(2,128)(2,1)}, u32[]{:S(2)}, u32[]{:S(2)}) async-start(bf16[2,128,24576]{1,0,2:T(2,128)(2,1)} %bitcast.379), calls=%async_computation | async-start | bytes 25165824 | tf_op jit(solution)/shard_map/all_to_all | solution.py:135
  158.3 124.6 %all_gather.3 = s32[4,4,8,4]{2,3,1,0:T(4,128)S(1)} all-gather(s32[1,4,8,4]{2,3,1,0:T(4,128)S(1)} %copy-done.13), channel_id=1, replica_groups=mesh['dp'=4,'grp'=32] {'dp'}, dimensions={0}, use_global_device_ids=true | all-gather | bytes 2560 | tf_op jit(solution)/shard_map/all_gather | solution.py:96
  283.7 13.0 %gather_fusion = bf16[512,4096]{1,0:T(8,128)(2,1)} fusion(bf16[1002,4096]{1,0:T(8,128)(2,1)} %param.43, s32[1024]{0:T(1024)S(1)} %pad_clamp_fusion), kind=kCustom, calls=%fused_computation | custom fusion | bytes 8390656 | tf_op jit(solution)/shard_map/jit(_take)/gather | solution.py:100
  296.7 7.6 %convert_select_fusion = f32[512,4096]{1,0:T(8,128)} fusion(bf16[512,4096]{1,0:T(8,128)(2,1)} %gather_fusion, pred[512]{0:T(512)(128)(4,1)S(1)} %compare_and_fusion.1, pred[512]{0:T(512)(128)(4,1)S(1)} %and.90), kind=kLoop, calls=%fused_computation.1 | loop fusion | flops 6291456 | bytes 12583936 | tf_op jit(solution)/shard_map/jit(_where)/select_n | solution.py:101
  304.4 157.6 %all-reduce.6 = bf16[512,4096]{1,0:T(8,128)(2,1)} all-reduce(f32[512,4096]{1,0:T(8,128)} %convert_select_fusion), channel_id=2, replica_groups=mesh['dp'=4,'grp'=32] {'dp','grp'}, use_global_device_ids=true, to_apply=%region_0.1.clone | all-reduce | flops 2097152 | bytes 12582912
  463.8 3.0 collective-permute-done
  466.9 1.6 collective-permute-start.1
  468.5 4.3 collective-permute-done.1
  472.8 1.3 collective-permute-start.2
  474.0 3.8 collective-permute-done.2
  479.0 5.1 copy.154
  484.1 3.7 fusion.277
  487.8 6.6 %copy.155 = bf16[1,32,128,512]{3,2,1,0:T(8,128)(2,1)} copy(bf16[1,32,128,512]{2,3,1,0:T(8,128)(2,1)} %get-tuple-element.209) | data formatting | bytes 8388608 | tf_op jit(solution)/shard_map/slice | solution.py:184
  494.4 6.5 %copy.162 = bf16[1,32,128,512]{3,2,1,0:T(8,128)(2,1)} copy(bf16[1,32,128,512]{2,3,1,0:T(8,128)(2,1)} %get-tuple-element.210) | data formatting | bytes 8388608 | tf_op jit(solution)/shard_map/slice | solution.py:184
  500.9 7.4 %copy.144 = bf16[2,128,24576]{1,2,0:T(8,128)(2,1)S(1)} copy(bf16[2,128,24576]{1,0,2:T(2,128)(2,1)} %all-to-all-done) | data formatting | bytes 25165824 | tf_op jit(solution)/shard_map/all_to_all | solution.py:135
  508.2 5.5 fusion.276
  513.8 8.6 %copy.145 = bf16[1,32,128,768]{3,2,1,0:T(8,128)(2,1)} copy(bf16[1,32,128,768]{2,3,1,0:T(8,128)(2,1)} %get-tuple-element.207) | data formatting | bytes 12582912 | tf_op jit(solution)/shard_map/slice | solution.py:156
  522.4 3.9 fusion.86
  529.2 2.5 fusion.285
  532.2 2.0 fusion.76
  535.8 8.7 %copy.156 = bf16[1,32,128,768]{3,2,1,0:T(8,128)(2,1)} copy(bf16[1,32,128,768]{2,3,1,0:T(8,128)(2,1)} %get-tuple-element.208) | data formatting | bytes 12582912 | tf_op jit(solution)/shard_map/slice | solution.py:156
  544.5 2.5 fusion.287
  547.6 2.2 fusion.77
  551.0 1.9 collective-permute-start.9
  552.9 2.5 fusion.289
  556.0 2.0 fusion.78
  560.4 2.6 collective-permute-start.4
  565.3 1.8 collective-permute-start.16
  569.7 2.0 collective-permute-start.11
  571.9 1.6 collective-permute-start.17
  575.0 1.9 collective-permute-done.17
  577.1 3.9 fusion.96
  581.2 2.5 fusion.291
  584.2 2.0 fusion.79
  589.4 2.5 fusion.299
  591.9 2.4 fusion.297
  594.4 2.3 collective-permute-start.22
  596.7 2.4 fusion.295
  599.0 1.9 collective-permute-done.22
  601.0 1.9 collective-permute-start.23
  602.9 3.3 collective-permute-done.23
  608.1 2.0 fusion.72
  611.3 1.3 collective-permute-start.6
  613.1 2.0 fusion.73
  617.6 2.0 fusion.74
  620.9 1.3 collective-permute-start.18
  622.2 2.5 fusion.293
  625.3 2.0 fusion.75
  629.3 2.3 collective-permute-start.7
  631.7 1.4 collective-permute-start.13
  633.1 2.3 collective-permute-start.19
  635.4 1.4 collective-permute-start.25
  636.8 1.7 collective-permute-start.8
  639.6 1.7 collective-permute-start.20
  642.0 1.3 collective-permute-start.26
  643.6 1.4 collective-permute-done.20
  645.0 2.0 collective-permute-done.26
  (230 shorter events, 38.4 us)
Async XLA Ops:
  0.0 463.6 %copy-start = (s32[1,4,8]{2,1,0:T(4,128)S(1)}, s32[1,4,8]{2,1,0:T(4,128)}, u32[]{:S(2)}) copy-start(s32[1,4,8]{2,1,0:T(4,128)} %param.42) | copy-start | bytes 388
  10.4 128.4 %all-to-all-start.1 = ((bf16[2,128,16384]{1,0,2:T(2,128)(2,1)}), bf16[2,128,16384]{1,0,2:T(2,128)(2,1)}, u32[]{:S(2)}, u32[]{:S(2)}) async-start(bf16[2,128,16384]{1,0,2:T(2,128)(2,1)} %bitcast.380), calls=%async_computation.1 | async-start | bytes 16777216 | tf_op jit(solution)/shard_map/all_to_all | solution.py:136
  19.8 1.9 copy-start.8
  19.8 2.5 slice-start.8
  147.9 10.5 %copy-start.13 = (s32[1,4,8,4]{2,3,1,0:T(4,128)S(1)}, s32[1,4,8,4]{2,3,1,0:T(4,128)}, u32[]{:S(2)}) copy-start(s32[1,4,8,4]{2,3,1,0:T(4,128)} %param.40) | copy-start | bytes 1540
  147.9 353.0 %all-to-all-start = ((bf16[2,128,24576]{1,0,2:T(2,128)(2,1)}), bf16[2,128,24576]{1,0,2:T(2,128)(2,1)}, u32[]{:S(2)}, u32[]{:S(2)}) async-start(bf16[2,128,24576]{1,0,2:T(2,128)(2,1)} %bitcast.379), calls=%async_computation | async-start | bytes 25165824 | tf_op jit(solution)/shard_map/all_to_all | solution.py:135
  304.4 159.4 %copy-start.12 = (f32[2,4096]{1,0:T(2,128)S(1)}, f32[2,4096]{1,0:T(2,128)}, u32[]{:S(2)}) copy-start(f32[2,4096]{1,0:T(2,128)} %param.44) | copy-start | bytes 98308
  462.8 4.0 collective-permute-start
  466.9 5.8 collective-permute-start.1
  472.8 5.0 collective-permute-start.2
  522.4 4.6 copy-start.2
  528.9 5.3 copy-start.5
  535.5 24.9 %collective-permute-start.3 = (f32[8,4096]{1,0:T(8,128)S(1)}, f32[8,4096]{1,0:T(8,128)S(1)}, u32[]{:S(2)}, u32[]{:S(2)}) collective-permute-start(f32[8,4096]{1,0:T(8,128)S(1)} %fusion.160), channel_id=1, source_target_pairs={{0,1},{1,0},{2,3},{3,2},{4,5},{5,4},{6,7},{7,6},{8,9},{9,8},{10,11... | collective-permute-start | bytes 393224 | tf_op jit(solution)/shard_map/ppermute | solution.py:26
  544.4 5.3 copy-start.6
  547.6 11.8 %slice-start.6 = ((s8[6291456]{0:T(1024)(128)(4,1)}), s8[4194304]{0:T(1024)(128)(4,1)S(1)}, s32[]{:S(2)}) async-start(s8[6291456]{0:T(1024)(128)(4,1)} %bitcast.367), calls=%async_computation.8 | async-start | bytes 8388608
  551.0 12.1 %collective-permute-start.9 = (f32[8,4096]{1,0:T(8,128)S(1)}, f32[8,4096]{1,0:T(8,128)S(1)}, u32[]{:S(2)}, u32[]{:S(2)}) collective-permute-start(f32[8,4096]{1,0:T(8,128)S(1)} %fusion.154), channel_id=1, source_target_pairs={{0,1},{1,0},{2,3},{3,2},{4,5},{5,4},{6,7},{7,6},{8,9},{9,8},{10,11... | collective-permute-start | bytes 393224 | tf_op jit(solution)/shard_map/ppermute | solution.py:26
  552.9 6.5 slice-start.7
  558.0 15.7 %slice-start = ((s8[6291456]{0:T(1024)(128)(4,1)}), s8[2097152]{0:T(1024)(128)(4,1)S(1)}, s32[]{:S(2)}) async-start(s8[6291456]{0:T(1024)(128)(4,1)} %bitcast.355), calls=%async_computation.2 | async-start | bytes 4194304
  559.2 14.5 %slice-start.1 = ((s8[6291456]{0:T(1024)(128)(4,1)}), s8[4194304]{0:T(1024)(128)(4,1)S(1)}, s32[]{:S(2)}) async-start(s8[6291456]{0:T(1024)(128)(4,1)} %bitcast.355), calls=%async_computation.3 | async-start | bytes 8388608
  559.2 6.1 collective-permute-start.15
  560.4 7.9 %collective-permute-start.4 = (f32[8,4096]{1,0:T(8,128)S(1)}, f32[8,4096]{1,0:T(8,128)S(1)}, u32[]{:S(2)}, u32[]{:S(2)}) collective-permute-start(f32[8,4096]{1,0:T(8,128)S(1)} %add.422), channel_id=1, source_target_pairs={{0,2},{2,0},{1,3},{3,1},{4,6},{6,4},{5,7},{7,5},{8,10},{10,8},{9,1... | collective-permute-start | bytes 393224 | tf_op jit(solution)/shard_map/ppermute | solution.py:26
  563.1 6.6 %collective-permute-start.10 = (f32[8,4096]{1,0:T(8,128)S(1)}, f32[8,4096]{1,0:T(8,128)S(1)}, u32[]{:S(2)}, u32[]{:S(2)}) collective-permute-start(f32[8,4096]{1,0:T(8,128)S(1)} %add.443), channel_id=1, source_target_pairs={{0,2},{2,0},{1,3},{3,1},{4,6},{6,4},{5,7},{7,5},{8,10},{10,8},{9,1... | collective-permute-start | bytes 393224 | tf_op jit(solution)/shard_map/ppermute | solution.py:26
  565.3 6.6 %collective-permute-start.16 = (f32[8,4096]{1,0:T(8,128)S(1)}, f32[8,4096]{1,0:T(8,128)S(1)}, u32[]{:S(2)}, u32[]{:S(2)}) collective-permute-start(f32[8,4096]{1,0:T(8,128)S(1)} %add.462), channel_id=1, source_target_pairs={{0,2},{2,0},{1,3},{3,1},{4,6},{6,4},{5,7},{7,5},{8,10},{10,8},{9,1... | collective-permute-start | bytes 393224 | tf_op jit(solution)/shard_map/ppermute | solution.py:26
  568.3 5.2 collective-permute-start.5
  569.7 5.1 collective-permute-start.11
  571.9 5.0 collective-permute-start.17
  577.1 11.1 %slice-start.2 = ((s8[6291456]{0:T(1024)(128)(4,1)}), s8[4194304]{0:T(1024)(128)(4,1)S(1)}, s32[]{:S(2)}) async-start(s8[6291456]{0:T(1024)(128)(4,1)} %bitcast.358), calls=%async_computation.4 | async-start | bytes 8388608
  581.0 6.4 copy-start.10
  581.0 5.2 copy-start.7
  581.2 7.1 %slice-start.3 = ((s8[6291456]{0:T(1024)(128)(4,1)}), s8[2097152]{0:T(1024)(128)(4,1)S(1)}, s32[]{:S(2)}) async-start(s8[6291456]{0:T(1024)(128)(4,1)} %bitcast.358), calls=%async_computation.5 | async-start | bytes 4194304
  587.4 6.9 %collective-permute-start.21 = (f32[8,4096]{1,0:T(8,128)S(1)}, f32[8,4096]{1,0:T(8,128)S(1)}, u32[]{:S(2)}, u32[]{:S(2)}) collective-permute-start(f32[8,4096]{1,0:T(8,128)S(1)} %fusion.142), channel_id=1, source_target_pairs={{0,1},{1,0},{2,3},{3,2},{4,5},{5,4},{6,7},{7,6},{8,9},{9,8},{10,11... | collective-permute-start | bytes 393224 | tf_op jit(solution)/shard_map/ppermute | solution.py:26
  588.2 1.1 slice-start.10
  588.2 18.2 %slice-start.4 = ((s8[6291456]{0:T(1024)(128)(4,1)}), s8[2097152]{0:T(1024)(128)(4,1)S(1)}, s32[]{:S(2)}) async-start(s8[6291456]{0:T(1024)(128)(4,1)} %bitcast.361), calls=%async_computation.6 | async-start | bytes 4194304
  589.3 17.1 %slice-start.5 = ((s8[6291456]{0:T(1024)(128)(4,1)}), s8[4194304]{0:T(1024)(128)(4,1)S(1)}, s32[]{:S(2)}) async-start(s8[6291456]{0:T(1024)(128)(4,1)} %bitcast.361), calls=%async_computation.7 | async-start | bytes 8388608
  594.4 6.6 %collective-permute-start.22 = (f32[8,4096]{1,0:T(8,128)S(1)}, f32[8,4096]{1,0:T(8,128)S(1)}, u32[]{:S(2)}, u32[]{:S(2)}) collective-permute-start(f32[8,4096]{1,0:T(8,128)S(1)} %add.481), channel_id=1, source_target_pairs={{0,2},{2,0},{1,3},{3,1},{4,6},{6,4},{5,7},{7,5},{8,10},{10,8},{9,1... | collective-permute-start | bytes 393224 | tf_op jit(solution)/shard_map/ppermute | solution.py:26
  601.0 5.3 collective-permute-start.23
  606.5 3.7 copy-start.3
  607.4 10.2 %copy-start.9 = (f32[8,768]{1,0:T(8,128)}, f32[8,768]{1,0:T(8,128)S(1)}, u32[]{:S(2)}) copy-start(f32[8,768]{1,0:T(8,128)S(1)} %fusion.100) | copy-start | bytes 73732
  607.4 5.7 copy-start.11
  611.3 18.0 %collective-permute-start.6 = (f32[8,4096]{1,0:T(8,128)S(1)}, f32[8,4096]{1,0:T(8,128)S(1)}, u32[]{:S(2)}, u32[]{:S(2)}) collective-permute-start(f32[8,4096]{1,0:T(8,128)S(1)} %fusion.157), channel_id=1, source_target_pairs={{0,1},{1,0},{2,3},{3,2},{4,5},{5,4},{6,7},{7,6},{8,9},{9,8},{10,11... | collective-permute-start | bytes 393224 | tf_op jit(solution)/shard_map/ppermute | solution.py:26
  616.3 15.3 %collective-permute-start.12 = (f32[8,4096]{1,0:T(8,128)S(1)}, f32[8,4096]{1,0:T(8,128)S(1)}, u32[]{:S(2)}, u32[]{:S(2)}) collective-permute-start(f32[8,4096]{1,0:T(8,128)S(1)} %fusion.151), channel_id=1, source_target_pairs={{0,1},{1,0},{2,3},{3,2},{4,5},{5,4},{6,7},{7,6},{8,9},{9,8},{10,11... | collective-permute-start | bytes 393224 | tf_op jit(solution)/shard_map/ppermute | solution.py:26
  617.6 4.5 slice-start.9
  620.9 12.2 %collective-permute-start.18 = (f32[8,4096]{1,0:T(8,128)S(1)}, f32[8,4096]{1,0:T(8,128)S(1)}, u32[]{:S(2)}, u32[]{:S(2)}) collective-permute-start(f32[8,4096]{1,0:T(8,128)S(1)} %fusion.145), channel_id=1, source_target_pairs={{0,1},{1,0},{2,3},{3,2},{4,5},{5,4},{6,7},{7,6},{8,9},{9,8},{10,11... | collective-permute-start | bytes 393224 | tf_op jit(solution)/shard_map/ppermute | solution.py:26
  622.2 5.2 copy-start.4
  625.3 22.4 %copy-start.1 = (s32[1,4,8]{2,1,0:T(4,128)S(1)}, s32[1,4,8]{2,1,0:T(4,128)}, u32[]{:S(2)}) copy-start(s32[1,4,8]{2,1,0:T(4,128)} %param.42) | copy-start | bytes 388
  628.5 6.8 %collective-permute-start.24 = (f32[8,4096]{1,0:T(8,128)S(1)}, f32[8,4096]{1,0:T(8,128)S(1)}, u32[]{:S(2)}, u32[]{:S(2)}) collective-permute-start(f32[8,4096]{1,0:T(8,128)S(1)} %fusion.139), channel_id=1, source_target_pairs={{0,1},{1,0},{2,3},{3,2},{4,5},{5,4},{6,7},{7,6},{8,9},{9,8},{10,11... | collective-permute-start | bytes 393224 | tf_op jit(solution)/shard_map/ppermute | solution.py:26
  629.3 7.4 %collective-permute-start.7 = (f32[8,4096]{1,0:T(8,128)S(1)}, f32[8,4096]{1,0:T(8,128)S(1)}, u32[]{:S(2)}, u32[]{:S(2)}) collective-permute-start(f32[8,4096]{1,0:T(8,128)S(1)} %add.431), channel_id=1, source_target_pairs={{0,2},{2,0},{1,3},{3,1},{4,6},{6,4},{5,7},{7,5},{8,10},{10,8},{9,1... | collective-permute-start | bytes 393224 | tf_op jit(solution)/shard_map/ppermute | solution.py:26
  631.7 6.9 %collective-permute-start.13 = (f32[8,4096]{1,0:T(8,128)S(1)}, f32[8,4096]{1,0:T(8,128)S(1)}, u32[]{:S(2)}, u32[]{:S(2)}) collective-permute-start(f32[8,4096]{1,0:T(8,128)S(1)} %add.452), channel_id=1, source_target_pairs={{0,2},{2,0},{1,3},{3,1},{4,6},{6,4},{5,7},{7,5},{8,10},{10,8},{9,1... | collective-permute-start | bytes 393224 | tf_op jit(solution)/shard_map/ppermute | solution.py:26
  633.1 6.6 %collective-permute-start.19 = (f32[8,4096]{1,0:T(8,128)S(1)}, f32[8,4096]{1,0:T(8,128)S(1)}, u32[]{:S(2)}, u32[]{:S(2)}) collective-permute-start(f32[8,4096]{1,0:T(8,128)S(1)} %add.471), channel_id=1, source_target_pairs={{0,2},{2,0},{1,3},{3,1},{4,6},{6,4},{5,7},{7,5},{8,10},{10,8},{9,1... | collective-permute-start | bytes 393224 | tf_op jit(solution)/shard_map/ppermute | solution.py:26
  635.4 6.6 %collective-permute-start.25 = (f32[8,4096]{1,0:T(8,128)S(1)}, f32[8,4096]{1,0:T(8,128)S(1)}, u32[]{:S(2)}, u32[]{:S(2)}) collective-permute-start(f32[8,4096]{1,0:T(8,128)S(1)} %add.490), channel_id=1, source_target_pairs={{0,2},{2,0},{1,3},{3,1},{4,6},{6,4},{5,7},{7,5},{8,10},{10,8},{9,1... | collective-permute-start | bytes 393224 | tf_op jit(solution)/shard_map/ppermute | solution.py:26
  636.8 6.4 collective-permute-start.8
  638.5 5.0 collective-permute-start.14
  639.6 5.4 collective-permute-start.20
  642.0 5.0 collective-permute-start.26
where the time goes:
time: 658 us; the launch traced here: 648 us
  blocking collectives  282 us (43%)
  waiting for transfers between devices  136 us (21%)
  local copies, waits for them, and re-layouts  96.3 us (15%)
  matrix products  62.6 us (10%)
  starting transfers between devices  57.3 us (9%)
  other arithmetic  12 us (2%)
    unnamed x1, blocking collectives  158 us
    all_gather x1, blocking collectives, body(): all_ids = lax.all_gather(token_ids, 'dp', axis=0, tiled=True).reshape(-1)  125 us
    all_to_all x1, waiting for transfers between devices, body(): lax.all_to_all(copied(output_slice_weight), 'grp', split_axis=2, concat_a...  111 us
    ppermute x27, starting transfers between devices, swapped(): return lax.ppermute(block, axis, route)  37.5 us
    ppermute x27, waiting for transfers between devices, swapped(): return lax.ppermute(block, axis, route)  25.6 us
    slice x3, local copies, waits for them, and re-layouts, body(): own_qkv[layer_no]  22.8 us
    dot_general x8, matrix products, attend_whole(): jnp.einsum('rgd,rjd->rgj', query_rows, cache_keys, preferred_element_type...  19.8 us
    broadcast_in_dim x3, local copies, waits for them, and re-layouts, copied(): jnp.broadcast_to(pieces[:, :, None], target)  19.5 us
  transfers between devices with their start and end apart: 29, of which 16 were waited for; matrix products, arithmetic and copies ran while one was open for 15% of the time, Pallas kernels for 0%

commit v1 on v0

v1 whole, which is shorter than its diff:
```python
import jax
import jax.numpy as jnp
from jax import lax
from jax.experimental import pallas as pl
from jax.experimental.pallas import tpu as pltpu
from jax.sharding import PartitionSpec as P

MODEL_WIDTH = 4096
QUERY_HEADS = 32
KEY_VALUE_HEADS = 8
HEAD_SIZE = 128
DECODER_LAYERS = 2
DECODE_STEPS = 4
REPLICA_ROWS = 8
ROPE_BASE = 500000.0
EPSILON = 1e-05

MESH = pl.DeviceIdType.MESH
SLOTS = 16
DP = 4
PLANES = 4
SLICES = 8
GRP = PLANES * SLICES
TOKENS = REPLICA_ROWS * DECODE_STEPS
ALL = PLANES * TOKENS
D = 128
QKV = 768
CACHE = 1024
FRESH_AT = CACHE - DECODE_STEPS
BF = jnp.bfloat16
F32 = jnp.float32


def ids_kernel(ids_ref, out_ref, land, send_sem, recv_sem):
    a, g = lax.axis_index("dp"), lax.axis_index("grp")
    barrier = pltpu.get_barrier_semaphore()
    for j in range(1, DP):
        pl.semaphore_signal(barrier, inc=1, device_id=((a + j) % DP, g), device_id_type=MESH)
    pl.semaphore_wait(barrier, DP - 1)
    copies = []
    for j in range(1, DP):
        copy = pltpu.make_async_remote_copy(
            src_ref=ids_ref,
            dst_ref=land.at[j],
            send_sem=send_sem.at[j],
            recv_sem=recv_sem.at[j],
            device_id=((a + j) % DP, g),
            device_id_type=MESH,
        )
        copy.start()
        copies.append(copy)
    out_ref[a] = ids_ref[...]
    for j in range(1, DP):
        copies[j - 1].wait()
        out_ref[(a - j + DP) % DP] = land[j]


def gather_ids(ids):
    return pl.pallas_call(
        ids_kernel,
        out_shape=jax.ShapeDtypeStruct((DP, 8, ALL), jnp.int32),
        in_specs=[pl.BlockSpec(memory_space=pltpu.VMEM)],
        out_specs=pl.BlockSpec(memory_space=pltpu.VMEM),
        scratch_shapes=[
            pltpu.VMEM((DP, 8, ALL), jnp.int32),
            pltpu.SemaphoreType.DMA((DP,)),
            pltpu.SemaphoreType.DMA((DP,)),
        ],
        compiler_params=pltpu.CompilerParams(collective_id=0, has_side_effects=True),
        name="gather_ids",
    )(jnp.broadcast_to(ids[None], (8, ALL)))


def main_kernel(
    rows_ref,
    idx_ref,
    extra_ref,
    gain_ref,
    cos_ref,
    sin_ref,
    len_ref,
    wq_ref,
    wo_ref,
    cache_ref,
    out_ref,
    cache_v,
    wqx,
    wox,
    ebuf,
    tbuf,
    dbuf,
    stream,
    p1s,
    p1r,
    p2s,
    p2r,
    qs,
    kvs,
    atts,
    p3s,
    p3r,
    p4s,
    p4r,
    pfs,
    pfr,
    cache_sem,
    w_send,
    w_recv,
    f_send,
    f_recv,
    e_send,
    e_recv,
    d_send,
    d_recv,
    p1_send,
    p1_recv,
    p2_send,
    p2_recv,
    p3_send,
    p3_recv,
    p4_send,
    p4_recv,
):
    a, g = lax.axis_index("dp"), lax.axis_index("grp")
    core = a % 2
    sibling = a + 1 - 2 * core
    z, t = g // SLICES, g % SLICES
    y, x = t // 4, t % 4

    def remote(src, dst, send_sem, recv_sem, a2, g2):
        return pltpu.make_async_remote_copy(
            src_ref=src,
            dst_ref=dst,
            send_sem=send_sem,
            recv_sem=recv_sem,
            device_id=(a2, g2),
            device_id_type=MESH,
        )

    def wait_bytes(ref, sem):
        pltpu.make_async_copy(ref, ref, sem).wait()

    def slice_at(j):
        return ((y + j // 4) % 2) * 4 + (x + j % 4) % 4

    for l in range(DECODER_LAYERS):
        pltpu.make_async_copy(cache_ref.at[l], cache_v.at[l], cache_sem.at[l]).start()

    barrier = pltpu.get_barrier_semaphore()

    def greet(j, c):
        pl.semaphore_signal(barrier, inc=1, device_id=(a, (g + j) % GRP), device_id_type=MESH)
        return c

    lax.fori_loop(1, GRP, greet, 0)
    for j in range(1, DP):
        pl.semaphore_signal(barrier, inc=1, device_id=((a + j) % DP, g), device_id_type=MESH)
    pl.semaphore_wait(barrier, GRP - 1 + DP - 1)

    def send_rows(j, c):
        g2 = ((z + j // SLICES) % PLANES) * SLICES + slice_at(j % SLICES)
        remote(rows_ref.at[g2], ebuf.at[g], e_send, e_recv, a, g2).start()
        return c

    lax.fori_loop(1, GRP, send_rows, 0)

    half = pl.ds(pl.multiple_of(core * 64, 64), 64)

    def qkv_pieces(l, t2):
        return (
            (
                wq_ref.at[l, half, pl.ds(pl.multiple_of(t2 * 512, 512), 512)],
                wqx.at[l, t, half, pl.ds(0, 512)],
            ),
            (
                wq_ref.at[l, half, pl.ds(pl.multiple_of(4096 + t2 * 128, 128), 128)],
                wqx.at[l, t, half, pl.ds(512, 128)],
            ),
            (
                wq_ref.at[l, half, pl.ds(pl.multiple_of(5120 + t2 * 128, 128), 128)],
                wqx.at[l, t, half, pl.ds(640, 128)],
            ),
        )

    def out_pieces(l, t2):
        return (
            (
                wo_ref.at[l, half, pl.ds(pl.multiple_of(t2 * 512, 512), 512)],
                wox.at[l, t, half, :],
            ),
        )

    def send_weights(l, kind):
        pieces = (qkv_pieces, out_pieces)[kind]

        def one(j, c):
            t2 = slice_at(j)
            for src, dst in pieces(l, t2):
                remote(src, dst, w_send.at[l, kind], w_recv.at[l, kind], a, z * SLICES + t2).start()
            return c

        lax.fori_loop(1, SLICES, one, 0)
        for src, dst in pieces(l, t):
            pltpu.make_async_copy(src, dst, w_recv.at[l, kind]).start()

    def forward_weights(l, kind):
        buf = (wqx, wox)[kind]
        wait_bytes(buf.at[l, :, half, :], w_recv.at[l, kind])
        remote(
            buf.at[l, :, half, :],
            buf.at[l, :, half, :],
            f_send.at[l, kind],
            f_recv.at[l, kind],
            sibling,
            g,
        ).start()

    def await_weights(l, kind):
        buf = (wqx, wox)[kind]
        wait_bytes(buf.at[l, :, half, :], f_recv.at[l, kind])

    send_weights(0, 0)
    ebuf[g] = rows_ref[g]
    kvs[...] = jnp.zeros_like(kvs)
    wait_bytes(ebuf.at[pl.ds(0, GRP - 1)], e_recv)
    table = ebuf[...].reshape(GRP * SLOTS, D)

    def picked(a2):
        want = idx_ref[pl.ds(pl.multiple_of(a2 * ALL, ALL), ALL), :]
        place = lax.broadcasted_iota(jnp.int32, (ALL, GRP * SLOTS), 1)
        chosen = jnp.where(place == want, 1.0, 0.0).astype(BF)
        return jnp.dot(chosen, table, preferred_element_type=F32)

    for j in range(1, DP):
        a2 = (a + j) % DP
        tbuf[j] = picked(a2).astype(BF)
        remote(tbuf.at[j], dbuf.at[j], d_send, d_recv, a2, g).start()
    send_weights(0, 1)
    mine = picked(a) + extra_ref[...]
    wait_bytes(dbuf.at[pl.ds(1, DP - 1)], d_recv)
    for j in range(1, DP):
        mine = mine + dbuf[j].astype(F32)
    stream[...] = mine

    row32 = lax.broadcasted_iota(jnp.int32, (TOKENS, ALL), 0)
    lane32 = lax.broadcasted_iota(jnp.int32, (TOKENS, ALL), 1)
    own_token = lane32 == row32 + z * TOKENS

    def split(value):
        high = value.astype(BF).astype(F32)
        return jnp.concatenate([high, value - high], axis=0).astype(BF)

    for l in range(DECODER_LAYERS):
        s = stream[...]
        square = s * s
        high = square.astype(BF)
        low = (square - high.astype(F32)).astype(BF)
        ones = jnp.ones((8, D), BF)
        contract = (((1,), (1,)), ((), ()))
        sums = lax.dot_general(ones, high, contract, preferred_element_type=F32)
        sums = sums + lax.dot_general(ones, low, contract, preferred_element_type=F32)
        p1s[l, 0:ALL, :] = (s * gain_ref[l]).astype(BF)
        p1s[l, ALL : ALL + 16, :] = split(sums)

        def send_stream(j, c):
            remote(
                p1s.at[l], p1r.at[l, t], p1_send.at[l], p1_recv.at[l], a, z * SLICES + slice_at(j)
            ).start()
            return c

        lax.fori_loop(1, SLICES, send_stream, 0)
        p1r[l, t] = p1s[l]
        forward_weights(l, 0)
        wait_bytes(p1r.at[l, pl.ds(0, SLICES - 1)], p1_recv.at[l])
        await_weights(l, 0)

        left = jnp.concatenate([p1r[l, j, 0:ALL, :] for j in range(SLICES)], axis=1)
        sums = jnp.zeros((8, ALL), F32)
        for j in range(SLICES):
            tile = p1r[l, j, ALL : ALL + 16, :].astype(F32)
            sums = sums + tile[0:8] + tile[8:16]
        projected = jnp.dot(
            left, wqx[l].reshape(SLICES * D, QKV), preferred_element_type=F32
        ).astype(BF)
        sums = split(sums)
        for r in range(PLANES):
            for c in range(QKV // D):
                p2s[l, r, c * TOKENS : (c + 1) * TOKENS, :] = projected[
                    r * TOKENS : (r + 1) * TOKENS, c * D : (c + 1) * D
                ]
            p2s[l, r, 192:208, :] = sums
        for j in range(1, PLANES):
            z2 = (z + j) % PLANES
            remote(
                p2s.at[l, z2], p2r.at[l, j], p2_send.at[l], p2_recv.at[l], a, z2 * SLICES + t
            ).start()
        forward_weights(l, 1)
        wait_bytes(p2r.at[l, pl.ds(1, PLANES - 1)], p2_recv.at[l])
        if l + 1 < DECODER_LAYERS:
            send_weights(l + 1, 0)
        total = p2s[l, z].astype(F32)
        for j in range(1, PLANES):
            total = total + p2r[l, j].astype(F32)

        line = total[192:193] + total[200:201]
        column = jnp.sum(
            jnp.where(own_token, jnp.broadcast_to(line, (TOKENS, ALL)), 0.0), axis=1, keepdims=True
        )
        factor = lax.rsqrt(column * (1.0 / MODEL_WIDTH) + EPSILON)
        cosine, sine = cos_ref[...], sin_ref[...]

        def rotated(block):
            return block * cosine + pltpu.roll(block, 64, 1) * sine

        for h in range(4):
            qs[h * TOKENS : (h + 1) * TOKENS, :] = rotated(
                total[h * TOKENS : (h + 1) * TOKENS] * factor
            )
        kvs[0, 96:128, :] = rotated(total[128:160] * factor)
        kvs[1, 96:128, :] = total[160:192] * factor
        pltpu.make_async_copy(cache_ref.at[l], cache_v.at[l], cache_sem.at[l]).wait()
        fresh_row = lax.broadcasted_iota(jnp.int32, (16, D), 0) >= 12
        place = lax.broadcasted_iota(jnp.int32, (16, CACHE), 1)
        step = lax.broadcasted_iota(jnp.int32, (16, CACHE), 0) % DECODE_STEPS
        fresh_live = (place >= FRESH_AT) & (place - FRESH_AT <= step)
        for b in range(REPLICA_ROWS):
            for k in range(2):
                old = cache_v[l, b, CACHE - 16 : CACHE, k * D : (k + 1) * D].astype(F32)
                new = kvs[k, pl.ds(b, 16, stride=8), :]
                cache_v[l, b, CACHE - 16 : CACHE, k * D : (k + 1) * D] = jnp.where(
                    fresh_row, new, old
                ).astype(BF)
        for b in range(REPLICA_ROWS):
            query = qs[pl.ds(b, 16, stride=8), :].astype(BF)
            scores = lax.dot_general(
                query, cache_v[l, b, :, 0:D], contract, preferred_element_type=F32
            ) * (HEAD_SIZE**-0.5)
            live = (place < len_ref[b]) | fresh_live
            scores = jnp.where(live, scores, -1e30)
            top = jnp.max(scores, axis=1, keepdims=True)
            power = jnp.exp(scores - top)
            whole = jnp.sum(power, axis=1, keepdims=True)
            value = jnp.dot(power.astype(BF), cache_v[l, b, :, D : 2 * D], preferred_element_type=F32)
            atts[pl.ds(b, 16, stride=8), :] = value / whole

        p3s[l] = atts[...].astype(BF)
        for j in range(1, PLANES):
            z2 = (z + j) % PLANES
            remote(
                p3s.at[l], p3r.at[l, z], p3_send.at[l], p3_recv.at[l], a, z2 * SLICES + t
            ).start()
        p3r[l, z] = p3s[l]
        await_weights(l, 1)
        wait_bytes(p3r.at[l, pl.ds(0, PLANES - 1)], p3_recv.at[l])
        if l + 1 < DECODER_LAYERS:
            send_weights(l + 1, 1)
        left = jnp.concatenate(
            [
                jnp.concatenate(
                    [p3r[l, r, h * TOKENS : (h + 1) * TOKENS, :] for r in range(PLANES)], axis=0
                )
                for h in range(4)
            ],
            axis=1,
        )

        def partial(t2):
            return lax.dot_general(left, wox[l, t2], contract, preferred_element_type=F32)

        if l + 1 < DECODER_LAYERS:

            for j in range(1, SLICES):
                t2 = slice_at(j)
                p4s[j] = partial(t2).astype(BF)
                remote(p4s.at[j], p4r.at[j], p4_send.at[0], p4_recv.at[0], a, z * SLICES + t2).start()
            s = stream[...] + partial(t)
            wait_bytes(p4r.at[pl.ds(1, SLICES - 1)], p4_recv.at[0])
            for j in range(1, SLICES):
                s = s + p4r[j].astype(F32)
            stream[...] = s
        else:
            for e in range(2):
                for k in range(4):
                    t2 = e * 4 + k
                    part = partial(t2)
                    part = part + jnp.where(t == t2, stream[...], 0.0)
                    part = part.astype(BF)
                    for r in range(PLANES):
                        pfs[r, e, :, k * D : (k + 1) * D] = part[r * TOKENS : (r + 1) * TOKENS]
                for j in range(PLANES):
                    r = (z + j) % PLANES
                    g2 = r * SLICES + 2 * z + e

                    @pl.when(g2 != g)
                    def _():
                        remote(
                            pfs.at[r, e], pfr.at[t], p4_send.at[1], p4_recv.at[1], a, g2
                        ).start()

                    @pl.when(g2 == g)
                    def _():
                        pltpu.make_async_copy(pfs.at[r, e], pfr.at[t], p4_recv.at[1]).start()

            wait_bytes(pfr, p4_recv.at[1])
            result = pfr[0].astype(F32)
            for j in range(1, SLICES):
                result = result + pfr[j].astype(F32)
            out_ref[...] = result.astype(BF)

    wait_bytes(ebuf.at[pl.ds(0, GRP - 1)], e_send)
    wait_bytes(dbuf.at[pl.ds(1, DP - 1)], d_send)
    for l in range(DECODER_LAYERS):
        for kind in range(2):
            buf = (wqx, wox)[kind]
            wait_bytes(buf.at[l, pl.ds(0, SLICES - 1), half, :], w_send.at[l, kind])
            wait_bytes(buf.at[l, :, half, :], f_send.at[l, kind])
        wait_bytes(p1r.at[l, pl.ds(0, SLICES - 1)], p1_send.at[l])
        wait_bytes(p2r.at[l, pl.ds(1, PLANES - 1)], p2_send.at[l])
        wait_bytes(p3r.at[l, pl.ds(0, PLANES - 1)], p3_send.at[l])
    wait_bytes(p4r.at[pl.ds(1, SLICES - 1)], p4_send.at[0])
    own_last = t // 2 == z

    @pl.when(own_last)
    def _():
        wait_bytes(pfr.at[pl.ds(0, SLICES - 1)], p4_send.at[1])

    @pl.when(jnp.logical_not(own_last))
    def _():
        wait_bytes(pfr, p4_send.at[1])


def decode(rows, idx, extra, gain, cosine, sine, lengths, wq, wo, cache):
    vmem = pl.BlockSpec(memory_space=pltpu.VMEM)
    hbm = pl.BlockSpec(memory_space=pl.ANY)
    layers = DECODER_LAYERS
    dma = pltpu.SemaphoreType.DMA
    return pl.pallas_call(
        main_kernel,
        out_shape=jax.ShapeDtypeStruct((TOKENS, 512), BF),
        in_specs=[
            vmem,
            vmem,
            vmem,
            vmem,
            vmem,
            vmem,
            pl.BlockSpec(memory_space=pltpu.SMEM),
            hbm,
            hbm,
            hbm,
        ],
        out_specs=vmem,
        scratch_shapes=[
            pltpu.VMEM((layers, REPLICA_ROWS, CACHE, 2 * D), BF),
            pltpu.VMEM((layers, SLICES, D, QKV), BF),
            pltpu.VMEM((layers, SLICES, D, 512), BF),
            pltpu.VMEM((GRP, SLOTS, D), BF),
            pltpu.VMEM((DP, ALL, D), BF),
            pltpu.VMEM((DP, ALL, D), BF),
            pltpu.VMEM((ALL, D), F32),
            pltpu.VMEM((layers, ALL + 16, D), BF),
            pltpu.VMEM((layers, SLICES, ALL + 16, D), BF),
            pltpu.VMEM((layers, PLANES, 208, D), BF),
            pltpu.VMEM((layers, PLANES, 208, D), BF),
            pltpu.VMEM((4 * TOKENS, D), F32),
            pltpu.VMEM((2, 16 * REPLICA_ROWS, D), F32),
            pltpu.VMEM((4 * TOKENS, D), F32),
            pltpu.VMEM((layers, 4 * TOKENS, D), BF),
            pltpu.VMEM((layers, PLANES, 4 * TOKENS, D), BF),
            pltpu.VMEM((SLICES, ALL, D), BF),
            pltpu.VMEM((SLICES, ALL, D), BF),
            pltpu.VMEM((PLANES, 2, TOKENS, 512), BF),
            pltpu.VMEM((SLICES, TOKENS, 512), BF),
            dma((layers,)),
            dma((layers, 2)),
            dma((layers, 2)),
            dma((layers, 2)),
            dma((layers, 2)),
            dma,
            dma,
            dma,
            dma,
            dma((layers,)),
            dma((layers,)),
            dma((layers,)),
            dma((layers,)),
            dma((layers,)),
            dma((layers,)),
            dma((2,)),
            dma((2,)),
        ],
        compiler_params=pltpu.CompilerParams(
            collective_id=1, has_side_effects=True, vmem_limit_bytes=40 * 1024 * 1024
        ),
        name="decode",
    )(rows, idx, extra, gain, cosine, sine, lengths, wq, wo, cache)


def body(
    token_ids,
    start_pos,
    cache_len,
    embed_table,
    norm_gain,
    query_key_value_weight,
    output_weight,
    key_value_cache,
):
    a, g = lax.axis_index("dp"), lax.axis_index("grp")
    z = g // SLICES
    me = a * GRP + g
    shard_rows = embed_table.shape[0]
    number = DP * ALL

    ids = gather_ids(token_ids[0].transpose(0, 2, 1).reshape(ALL))[:, 0, :].reshape(number)
    owner = ids // shard_rows
    order = jnp.arange(number, dtype=jnp.int32)
    same_id = ids[:, None] == ids[None, :]
    first = jnp.min(jnp.where(same_id, order[None, :], number), axis=1)
    is_first = first == order
    before = is_first[None, :] & (owner[:, None] == owner[None, :]) & (order[None, :] < first[:, None])
    slot = jnp.sum(before.astype(jnp.int32), axis=1)
    holds = (
        is_first[None, :]
        & (owner[None, :] == me)
        & (slot[None, :] == jnp.arange(SLOTS, dtype=jnp.int32)[:, None])
    )
    local = jnp.sum(jnp.where(holds, ids[None, :] - me * shard_rows, 0), axis=1)
    rows = jnp.take(embed_table, local, axis=0, mode="clip")
    rows = rows.reshape(SLOTS, GRP, D).transpose(1, 0, 2)
    idx = jnp.where((owner // GRP == a) & (slot < SLOTS), (owner % GRP) * SLOTS + slot, -1)

    def overflow(_):
        late = (owner == me) & (slot >= SLOTS)
        more = jnp.take(embed_table, jnp.where(late, ids - me * shard_rows, 0), axis=0, mode="clip")
        more = jnp.where(late[:, None], more.astype(F32), 0.0).reshape(DP, ALL, GRP, D)
        more = lax.psum_scatter(more, "dp", scatter_dimension=0, tiled=False)
        return lax.psum_scatter(more, "grp", scatter_dimension=1, tiled=False)

    extra = lax.cond(
        jnp.max(slot) >= SLOTS, overflow, lambda _: jnp.zeros((ALL, D), F32), jnp.int32(0)
    )

    lengths = lax.dynamic_index_in_dim(cache_len[0], z, 0, keepdims=False)
    starts = lax.dynamic_index_in_dim(start_pos[0], z, 0, keepdims=False)
    position = (starts[None, :] + jnp.arange(DECODE_STEPS, dtype=jnp.int32)[:, None]).reshape(TOKENS)
    exponent = jnp.arange(HEAD_SIZE // 2, dtype=F32) * (2.0 / HEAD_SIZE)
    frequency = jnp.power(F32(ROPE_BASE), -exponent)
    angles = position.astype(F32)[:, None] * frequency
    cosine, sine = jnp.cos(angles), jnp.sin(angles)
    cosine = jnp.concatenate([cosine, cosine], axis=1)
    sine = jnp.concatenate([-sine, sine], axis=1)
    gain = lax.dynamic_slice_in_dim(norm_gain, g * D, D, 1).reshape(DECODER_LAYERS, 1, D)

    out = decode(
        rows,
        idx.reshape(number, 1),
        extra,
        gain,
        cosine,
        sine,
        lengths,
        query_key_value_weight,
        output_weight,
        key_value_cache.reshape(DECODER_LAYERS, REPLICA_ROWS, CACHE, 2 * D),
    )
    return out.reshape(DECODE_STEPS, REPLICA_ROWS, 512).transpose(1, 0, 2)[:, None]


def solution(mesh):
    return jax.shard_map(
        body,
        mesh=mesh,
        in_specs=(
            P("dp", None, None, None),
            P("dp", None, None),
            P("dp", None, None),
            P(("dp", "grp"), None),
            P(),
            P(None, "grp", None),
            P(None, "grp", None),
            P(None, "dp", "grp", None, None),
        ),
        out_specs=P("dp", "grp", None, None),
        check_vma=False,
    )
```

time: 658 us -> 132 us (0.20); the launches traced: 648 us -> 131 us
  blocking collectives: 282 us -> 0 us
  waiting for transfers between devices: 136 us -> 0 us
  Pallas kernels: 0 us -> 96.7 us
  local copies, waits for them, and re-layouts: 96.3 us -> 15.6 us
  matrix products: 62.6 us -> 0 us
  starting transfers between devices: 57.3 us -> 0 us
  between operations: 0.98 us -> 14.1 us
  other arithmetic: 12 us -> 4.69 us
    unnamed x1 -> x0, blocking collectives: 158 us -> none
    all_gather x1 -> x0, blocking collectives: 125 us -> none  [body(): all_ids = lax.all_gather(token_ids, 'dp', axis=0, tiled=True).reshape(-1)]
    all_to_all x2 -> x0, waiting for transfers between devices: 111 us -> none  [the longest x1 111 us: body(): lax.all_to_all(copied(output_slice_weight), 'grp', split_axis=2, concat_a...]
    pallas_call x0 -> x2, Pallas kernels: none -> 96.7 us  [the longest x1 90.2 us: decode(): pl.pallas_call(main_kernel, out_shape=jax.ShapeDtypeStruct((TOKENS, 512),...]
    dot_general x48 -> x0, matrix products: 62.6 us -> none  [the longest x8 19.8 us: attend_whole(): jnp.einsum('rgd,rjd->rgj', query_rows, cache_keys, preferred_element_type...]
    slice x21 -> x0, local copies, waits for them, and re-layouts: 40.8 us -> none  [the longest x3 22.8 us: body(): own_qkv[layer_no]]
    ppermute x27 -> x0, starting transfers between devices: 37.5 us -> none  [swapped(): return lax.ppermute(block, axis, route)]
    ppermute x27 -> x0, waiting for transfers between devices: 25.6 us -> none  [swapped(): return lax.ppermute(block, axis, route)]
  transfers between devices with their start and end apart: 29 -> 0, of which waited for: 16 -> 0; matrix products, arithmetic and copies ran while one was open for 15% -> 0% of each run, Pallas kernels for 0% -> 0%
where the time goes in v1:
time: 132 us; the launch traced here: 131 us
  Pallas kernels  96.7 us (73%)
  local copies, waits for them, and re-layouts  15.6 us (12%)
  between operations  14.1 us (11%)
  other arithmetic  4.69 us (4%)
    pallas_call x1, Pallas kernels, decode(): pl.pallas_call(main_kernel, out_shape=jax.ShapeDtypeStruct((TOKENS, 512),...  90.2 us
    pallas_call x1, Pallas kernels, gather_ids(): pl.pallas_call(ids_kernel, out_shape=jax.ShapeDtypeStruct((DP, 8, ALL), j...  6.47 us
    gather x1, local copies, waits for them, and re-layouts, body(): rows = jnp.take(embed_table, local, axis=0, mode='clip')  5.28 us
    unnamed x8, local copies, waits for them, and re-layouts  4.98 us

profile of v1, /device:TPU:8, one launch (start us, length us, event | category | flops | bytes accessed | tf_op | source)
XLA Modules:
  0.0 131.2 jit_solution(18139143349283898133)
XLA Ops:
  6.5 0.0 copy-start
  6.5 0.8 broadcast_in_dim.78
  7.3 0.0 copy-done
  7.4 0.7 fusion.11
  8.1 0.1 convert_element_type.26
  8.2 0.6 broadcast_in_dim.79.ids_ref
  8.8 6.5 %gather_ids.1 = s32[4,8,128]{2,1,0:T(8,128)} custom-call(s32[8,128]{1,0:T(8,128)} %broadcast_in_dim.79.ids_ref), custom_call_target="tpu_custom_call" | custom-call | tf_op jit(solution)/shard_map/gather_ids/pallas_call | solution.py:59
  15.3 0.7 and_bitcast_fusion
  16.0 0.7 divide_bitcast_fusion
  16.7 0.3 select_reduce_fusion
  17.0 0.5 convert_reduce_fusion
  17.5 0.6 reduce_max.9
  18.8 0.1 select_reduce_fusion.1
  19.0 0.1 fusion.9
  19.1 0.1 pad_maximum_fusion.1.sin_ref
  19.2 0.1 pad_maximum_fusion.cos_ref
  19.3 0.0 copy-start.2
  19.3 0.7 conditional.1
  19.3 0.6 broadcast.230
  19.9 0.2 copy.22
  20.1 5.3 %gather_fusion.1 = bf16[16,4096]{1,0:T(8,128)(2,1)S(1)} fusion(bf16[1002,4096]{1,0:T(8,128)(2,1)} %param.13, s32[1024]{0:T(1024)S(1)} %pad_clamp_fusion.1), kind=kCustom, calls=%fused_computation.1 | custom fusion | bytes 262208 | tf_op jit(solution)/shard_map/jit(_take)/gather | solution.py:529
  25.4 0.9 copy.21
  26.3 0.8 copy.24
  27.1 1.3 %fusion.6.idx_ref = s32[512,1]{1,0:T(8,128)S(1)} fusion(s32[512,1]{1,0:T(8,128)} %copy.24, pred[512,1]{1,0:T(8,128)(4,1)S(1)} %copy.22, s32[512,1]{1,0:T(8,128)} %copy.21, s32[]{:T(128)S(6)} %axis_index.23), kind=kLoop, calls=%fused_computation.25 | loop fusion | flops 13824 | bytes 6660 | tf_op jit(solution)/shard_map/jit(_where)/select_n | solution.py:531
  28.5 0.0 copy-done.2
  28.5 0.0 copy-start.1
  28.5 3.4 %copy-done.1 = bf16[2,8,1,1024,256]{4,3,2,1,0:T(8,128)(2,1)S(1)} copy-done((bf16[2,8,1,1024,256]{4,3,2,1,0:T(8,128)(2,1)S(1)}, bf16[2,8,1,1024,256]{4,3,2,1,0:T(8,128)(2,1)}, u32[]{:S(2)}) %copy-start.1) | copy-done | bytes 8388632
  31.9 0.0 copy-start.3
  31.9 1.6 %copy-done.3 = bf16[2,128,4096]{2,1,0:T(8,128)(2,1)S(1)} copy-done((bf16[2,128,4096]{2,1,0:T(8,128)(2,1)S(1)}, bf16[2,128,4096]{2,1,0:T(8,128)(2,1)}, u32[]{:S(2)}) %copy-start.3) | copy-done | bytes 2097176
  33.5 90.2 %decode.1 = bf16[32,512]{1,0:T(8,128)(2,1)S(1)} custom-call(bf16[32,16,128]{2,1,0:T(8,128)(2,1)S(1)} %bitcast_bitcast_fusion.rows_ref, s32[512,1]{1,0:T(8,128)S(1)} %fusion.6.idx_ref, f32[128,128]{1,0:T(8,128)} %get-tuple-element.56.extra_ref, f32[2,1,128]{2,1,0:T(1,128)S(1)} %bitcast.37, f32[32,128]{1,0:T(8,128)S(1)} %pad_maximum_fusion.cos_ref, ...), custom_call_target="tpu_custom_call" | custom-call | tf_op jit(solution)/shard_map/decode/pallas_call | solution.py:437
  123.7 0.6 copy.32
  (8 shorter events, 0.1 us)
Async XLA Ops:
  6.5 0.8 copy-start
  19.3 9.2 %copy-start.2 = (bf16[2,128,6144]{2,1,0:T(8,128)(2,1)S(1)}, bf16[2,128,6144]{2,1,0:T(8,128)(2,1)}, u32[]{:S(2)}) copy-start(bf16[2,128,6144]{2,1,0:T(8,128)(2,1)} %wq_ref.1) | copy-start | bytes 9437188
  28.5 3.4 %copy-start.1 = (bf16[2,8,1,1024,256]{4,3,2,1,0:T(8,128)(2,1)S(1)}, bf16[2,8,1,1024,256]{4,3,2,1,0:T(8,128)(2,1)}, u32[]{:S(2)}) copy-start(bf16[2,8,1,1024,256]{4,3,2,1,0:T(8,128)(2,1)} %param.17) | copy-start | bytes 25165828
  31.9 1.6 %copy-start.3 = (bf16[2,128,4096]{2,1,0:T(8,128)(2,1)S(1)}, bf16[2,128,4096]{2,1,0:T(8,128)(2,1)}, u32[]{:S(2)}) copy-start(bf16[2,128,4096]{2,1,0:T(8,128)(2,1)} %wo_ref.1) | copy-start | bytes 6291460

commit v2 on v1

--- a/solution.py
+++ b/solution.py
@@ -101,8 +101,8 @@
     p3r,
     p4s,
     p4r,
-    pfs,
-    pfr,
+    last,
+    final,
     cache_sem,
     w_send,
     w_recv,
@@ -120,6 +120,8 @@
     p3_recv,
     p4_send,
     p4_recv,
+    o_send,
+    o_recv,
 ):
     a, g = lax.axis_index("dp"), lax.axis_index("grp")
     core = a % 2
@@ -367,45 +369,36 @@
         def partial(t2):
             return lax.dot_general(left, wox[l, t2], contract, preferred_element_type=F32)
 
-        if l + 1 < DECODER_LAYERS:
-
-            for j in range(1, SLICES):
-                t2 = slice_at(j)
-                p4s[j] = partial(t2).astype(BF)
-                remote(p4s.at[j], p4r.at[j], p4_send.at[0], p4_recv.at[0], a, z * SLICES + t2).start()
-            s = stream[...] + partial(t)
-            wait_bytes(p4r.at[pl.ds(1, SLICES - 1)], p4_recv.at[0])
-            for j in range(1, SLICES):
-                s = s + p4r[j].astype(F32)
-            stream[...] = s
-        else:
-            for e in range(2):
-                for k in range(4):
-                    t2 = e * 4 + k
-                    part = partial(t2)
-                    part = part + jnp.where(t == t2, stream[...], 0.0)
-                    part = part.astype(BF)
-                    for r in range(PLANES):
-                        pfs[r, e, :, k * D : (k + 1) * D] = part[r * TOKENS : (r + 1) * TOKENS]
-                for j in range(PLANES):
-                    r = (z + j) % PLANES
-                    g2 = r * SLICES + 2 * z + e
-
-                    @pl.when(g2 != g)
-                    def _():
-                        remote(
-                            pfs.at[r, e], pfr.at[t], p4_send.at[1], p4_recv.at[1], a, g2
-                        ).start()
-
-                    @pl.when(g2 == g)
-                    def _():
-                        pltpu.make_async_copy(pfs.at[r, e], pfr.at[t], p4_recv.at[1]).start()
-
-            wait_bytes(pfr, p4_recv.at[1])
-            result = pfr[0].astype(F32)
-            for j in range(1, SLICES):
-                result = result + pfr[j].astype(F32)
-            out_ref[...] = result.astype(BF)
+        for j in range(1, SLICES):
+            t2 = slice_at(j)
+            p4s[l, j] = partial(t2).astype(BF)
+            remote(
+                p4s.at[l, j], p4r.at[l, j], p4_send.at[l], p4_recv.at[l], a, z * SLICES + t2
+            ).start()
+        s = stream[...] + partial(t)
+        wait_bytes(p4r.at[l, pl.ds(1, SLICES - 1)], p4_recv.at[l])
+        for j in range(1, SLICES):
+            s = s + p4r[l, j].astype(F32)
+        stream[...] = s
+
+    last[...] = stream[...].astype(BF)
+    home = g // 4
+    for j in range(PLANES):
+        r = (z + j) % PLANES
+        g2 = r * SLICES + home
+        tokens = last.at[pl.ds(pl.multiple_of(r * TOKENS, TOKENS), TOKENS), :]
+
+        @pl.when(g2 != g)
+        def _():
+            remote(tokens, final.at[g % 4], o_send, o_recv, a, g2).start()
+
+        @pl.when(g2 == g)
+        def _():
+            pltpu.make_async_copy(tokens, final.at[g % 4], o_recv).start()
+
+    wait_bytes(final, o_recv)
+    for k in range(4):
+        out_ref[:, k * D : (k + 1) * D] = final[k]
 
     wait_bytes(ebuf.at[pl.ds(0, GRP - 1)], e_send)
     wait_bytes(dbuf.at[pl.ds(1, DP - 1)], d_send)
@@ -417,16 +410,15 @@
         wait_bytes(p1r.at[l, pl.ds(0, SLICES - 1)], p1_send.at[l])
         wait_bytes(p2r.at[l, pl.ds(1, PLANES - 1)], p2_send.at[l])
         wait_bytes(p3r.at[l, pl.ds(0, PLANES - 1)], p3_send.at[l])
-    wait_bytes(p4r.at[pl.ds(1, SLICES - 1)], p4_send.at[0])
-    own_last = t // 2 == z
-
-    @pl.when(own_last)
+        wait_bytes(p4r.at[l, pl.ds(1, SLICES - 1)], p4_send.at[l])
+
+    @pl.when(home == t)
     def _():
-        wait_bytes(pfr.at[pl.ds(0, SLICES - 1)], p4_send.at[1])
-
-    @pl.when(jnp.logical_not(own_last))
+        wait_bytes(final.at[pl.ds(0, PLANES - 1)], o_send)
+
+    @pl.when(home != t)
     def _():
-        wait_bytes(pfr, p4_send.at[1])
+        wait_bytes(final, o_send)
 
 
 def decode(rows, idx, extra, gain, cosine, sine, lengths, wq, wo, cache):
@@ -467,10 +459,10 @@
             pltpu.VMEM((4 * TOKENS, D), F32),
             pltpu.VMEM((layers, 4 * TOKENS, D), BF),
             pltpu.VMEM((layers, PLANES, 4 * TOKENS, D), BF),
-            pltpu.VMEM((SLICES, ALL, D), BF),
-            pltpu.VMEM((SLICES, ALL, D), BF),
-            pltpu.VMEM((PLANES, 2, TOKENS, 512), BF),
-            pltpu.VMEM((SLICES, TOKENS, 512), BF),
+            pltpu.VMEM((layers, SLICES, ALL, D), BF),
+            pltpu.VMEM((layers, SLICES, ALL, D), BF),
+            pltpu.VMEM((ALL, D), BF),
+            pltpu.VMEM((4, TOKENS, D), BF),
             dma((layers,)),
             dma((layers, 2)),
             dma((layers, 2)),
@@ -486,8 +478,10 @@
             dma((layers,)),
             dma((layers,)),
             dma((layers,)),
-            dma((2,)),
-            dma((2,)),
+            dma((layers,)),
+            dma((layers,)),
+            dma,
+            dma,
         ],
         compiler_params=pltpu.CompilerParams(
             collective_id=1, has_side_effects=True, vmem_limit_bytes=40 * 1024 * 1024
@@ -533,9 +527,10 @@
     def overflow(_):
         late = (owner == me) & (slot >= SLOTS)
         more = jnp.take(embed_table, jnp.where(late, ids - me * shard_rows, 0), axis=0, mode="clip")
-        more = jnp.where(late[:, None], more.astype(F32), 0.0).reshape(DP, ALL, GRP, D)
-        more = lax.psum_scatter(more, "dp", scatter_dimension=0, tiled=False)
-        return lax.psum_scatter(more, "grp", scatter_dimension=1, tiled=False)
+        more = jnp.where(late[:, None], more, jnp.zeros_like(more)).reshape(DP, ALL, GRP, D)
+        more = more.transpose(0, 2, 1, 3).reshape(DP * GRP, ALL, D)
+        more = lax.all_to_all(more, ("dp", "grp"), split_axis=0, concat_axis=0, tiled=True)
+        return jnp.sum(more.astype(F32), axis=0)
 
     extra = lax.cond(
         jnp.max(slot) >= SLOTS, overflow, lambda _: jnp.zeros((ALL, D), F32), jnp.int32(0)

time: 132 us -> 118 us (0.89)
  between operations: 14.1 us -> 0.77 us
where the time goes in v2:
time: 118 us
  Pallas kernels  96.5 us (82%)
  local copies, waits for them, and re-layouts  15.5 us (13%)
  other arithmetic  4.72 us (4%)
    pallas_call x1, Pallas kernels, decode(): pl.pallas_call(main_kernel, out_shape=jax.ShapeDtypeStruct((TOKENS, 512),...  90 us
    pallas_call x1, Pallas kernels, gather_ids(): pl.pallas_call(ids_kernel, out_shape=jax.ShapeDtypeStruct((DP, 8, ALL), j...  6.47 us
    gather x1, local copies, waits for them, and re-layouts, body(): rows = jnp.take(embed_table, local, axis=0, mode='clip')  5.15 us
    unnamed x8, local copies, waits for them, and re-layouts  4.98 us

profile of v2, /device:TPU:8, one launch (start us, length us, event | category | flops | bytes accessed | tf_op | source)
XLA Modules:
  0.0 117.6 jit_solution(7396036141326721707)
XLA Ops:
  0.0 0.0 copy-start
  0.0 0.8 broadcast_in_dim.74
  0.8 0.0 copy-done
  0.8 0.7 fusion.11
  1.6 0.1 convert_element_type.22
  1.6 0.6 broadcast_in_dim.75.ids_ref
  2.2 6.5 %gather_ids.1 = s32[4,8,128]{2,1,0:T(8,128)} custom-call(s32[8,128]{1,0:T(8,128)} %broadcast_in_dim.75.ids_ref), custom_call_target="tpu_custom_call" | custom-call | tf_op jit(solution)/shard_map/gather_ids/pallas_call | solution.py:59
  8.7 0.7 and_bitcast_fusion
  9.5 0.7 divide_bitcast_fusion
  10.2 0.3 select_reduce_fusion
  10.5 0.5 convert_reduce_fusion.1
  11.0 0.6 reduce_max.9
  12.3 0.1 select_reduce_fusion.1
  12.4 0.1 fusion.9
  12.6 0.1 pad_maximum_fusion.1.sin_ref
  12.7 0.1 pad_maximum_fusion.cos_ref
  12.7 0.0 copy-start.2
  12.7 0.2 conditional.1
  12.9 0.8 copy.21
  13.7 5.2 %gather_fusion.1 = bf16[16,4096]{1,0:T(8,128)(2,1)S(1)} fusion(bf16[1002,4096]{1,0:T(8,128)(2,1)} %param.13, s32[1024]{0:T(1024)S(1)} %pad_clamp_fusion.1), kind=kCustom, calls=%fused_computation.1 | custom fusion | bytes 262208 | tf_op jit(solution)/shard_map/jit(_take)/gather | solution.py:523
  18.9 0.9 copy.20
  19.8 0.8 copy.23
  20.6 1.4 %fusion.6.idx_ref = s32[512,1]{1,0:T(8,128)S(1)} fusion(s32[512,1]{1,0:T(8,128)} %copy.23, pred[512,1]{1,0:T(8,128)(4,1)} %copy.21, s32[512,1]{1,0:T(8,128)} %copy.20, s32[]{:T(128)S(6)} %axis_index.23), kind=kLoop, calls=%fused_computation.25 | loop fusion | flops 13824 | bytes 6660 | tf_op jit(solution)/shard_map/jit(_where)/select_n | solution.py:525
  22.0 0.0 copy-done.2
  22.0 0.0 copy-start.1
  22.0 3.4 %copy-done.1 = bf16[2,8,1,1024,256]{4,3,2,1,0:T(8,128)(2,1)S(1)} copy-done((bf16[2,8,1,1024,256]{4,3,2,1,0:T(8,128)(2,1)S(1)}, bf16[2,8,1,1024,256]{4,3,2,1,0:T(8,128)(2,1)}, u32[]{:S(2)}) %copy-start.1) | copy-done | bytes 8388632
  25.4 0.0 copy-start.3
  25.4 1.6 %copy-done.3 = bf16[2,128,4096]{2,1,0:T(8,128)(2,1)S(1)} copy-done((bf16[2,128,4096]{2,1,0:T(8,128)(2,1)S(1)}, bf16[2,128,4096]{2,1,0:T(8,128)(2,1)}, u32[]{:S(2)}) %copy-start.3) | copy-done | bytes 2097176
  27.0 90.0 %decode.1 = bf16[32,512]{1,0:T(8,128)(2,1)S(1)} custom-call(bf16[32,16,128]{2,1,0:T(8,128)(2,1)S(1)} %bitcast_bitcast_fusion.rows_ref, s32[512,1]{1,0:T(8,128)S(1)} %fusion.6.idx_ref, f32[128,128]{1,0:T(8,128)S(1)} %get-tuple-element.56.extra_ref, f32[2,1,128]{2,1,0:T(1,128)S(1)} %bitcast.37, f32[32,128]{1,0:T(8,128)S(1)} %pad_maximum_fusion.cos_ref, ...), custom_call_target="tpu_custom_call" | custom-call | tf_op jit(solution)/shard_map/decode/pallas_call | solution.py:429
  117.0 0.6 copy.31
  (9 shorter events, 0.1 us)
Async XLA Ops:
  0.0 0.8 copy-start
  12.7 9.3 %copy-start.2 = (bf16[2,128,6144]{2,1,0:T(8,128)(2,1)S(1)}, bf16[2,128,6144]{2,1,0:T(8,128)(2,1)}, u32[]{:S(2)}) copy-start(bf16[2,128,6144]{2,1,0:T(8,128)(2,1)} %wq_ref.1) | copy-start | bytes 9437188
  22.0 3.4 %copy-start.1 = (bf16[2,8,1,1024,256]{4,3,2,1,0:T(8,128)(2,1)S(1)}, bf16[2,8,1,1024,256]{4,3,2,1,0:T(8,128)(2,1)}, u32[]{:S(2)}) copy-start(bf16[2,8,1,1024,256]{4,3,2,1,0:T(8,128)(2,1)} %param.17) | copy-start | bytes 25165828
  25.4 1.6 %copy-start.3 = (bf16[2,128,4096]{2,1,0:T(8,128)(2,1)S(1)}, bf16[2,128,4096]{2,1,0:T(8,128)(2,1)}, u32[]{:S(2)}) copy-start(bf16[2,128,4096]{2,1,0:T(8,128)(2,1)} %wo_ref.1) | copy-start | bytes 6291460

commit v3 on v2

--- a/solution.py
+++ b/solution.py
@@ -26,54 +26,15 @@
 D = 128
 QKV = 768
 CACHE = 1024
+SHARD = 1002
+SHARD_WHOLE = 992
 FRESH_AT = CACHE - DECODE_STEPS
 BF = jnp.bfloat16
 F32 = jnp.float32
 
 
-def ids_kernel(ids_ref, out_ref, land, send_sem, recv_sem):
-    a, g = lax.axis_index("dp"), lax.axis_index("grp")
-    barrier = pltpu.get_barrier_semaphore()
-    for j in range(1, DP):
-        pl.semaphore_signal(barrier, inc=1, device_id=((a + j) % DP, g), device_id_type=MESH)
-    pl.semaphore_wait(barrier, DP - 1)
-    copies = []
-    for j in range(1, DP):
-        copy = pltpu.make_async_remote_copy(
-            src_ref=ids_ref,
-            dst_ref=land.at[j],
-            send_sem=send_sem.at[j],
-            recv_sem=recv_sem.at[j],
-            device_id=((a + j) % DP, g),
-            device_id_type=MESH,
-        )
-        copy.start()
-        copies.append(copy)
-    out_ref[a] = ids_ref[...]
-    for j in range(1, DP):
-        copies[j - 1].wait()
-        out_ref[(a - j + DP) % DP] = land[j]
-
-
-def gather_ids(ids):
-    return pl.pallas_call(
-        ids_kernel,
-        out_shape=jax.ShapeDtypeStruct((DP, 8, ALL), jnp.int32),
-        in_specs=[pl.BlockSpec(memory_space=pltpu.VMEM)],
-        out_specs=pl.BlockSpec(memory_space=pltpu.VMEM),
-        scratch_shapes=[
-            pltpu.VMEM((DP, 8, ALL), jnp.int32),
-            pltpu.SemaphoreType.DMA((DP,)),
-            pltpu.SemaphoreType.DMA((DP,)),
-        ],
-        compiler_params=pltpu.CompilerParams(collective_id=0, has_side_effects=True),
-        name="gather_ids",
-    )(jnp.broadcast_to(ids[None], (8, ALL)))
-
-
 def main_kernel(
-    rows_ref,
-    idx_ref,
+    ids_ref,
     extra_ref,
     gain_ref,
     cos_ref,
@@ -82,8 +43,16 @@
     wq_ref,
     wo_ref,
     cache_ref,
+    embed_ref,
     out_ref,
+    all_ref,
+    most_ref,
     cache_v,
+    shard_v,
+    land,
+    tail_v,
+    rows_v,
+    chosen_v,
     wqx,
     wox,
     ebuf,
@@ -122,6 +91,9 @@
     p4_recv,
     o_send,
     o_recv,
+    i_send,
+    i_recv,
+    s_sem,
 ):
     a, g = lax.axis_index("dp"), lax.axis_index("grp")
     core = a % 2
@@ -145,6 +117,8 @@
     def slice_at(j):
         return ((y + j // 4) % 2) * 4 + (x + j % 4) % 4
 
+    shard_copy = pltpu.make_async_copy(embed_ref, shard_v, s_sem)
+    shard_copy.start()
     for l in range(DECODER_LAYERS):
         pltpu.make_async_copy(cache_ref.at[l], cache_v.at[l], cache_sem.at[l]).start()
 
@@ -159,12 +133,9 @@
         pl.semaphore_signal(barrier, inc=1, device_id=((a + j) % DP, g), device_id_type=MESH)
     pl.semaphore_wait(barrier, GRP - 1 + DP - 1)
 
-    def send_rows(j, c):
-        g2 = ((z + j // SLICES) % PLANES) * SLICES + slice_at(j % SLICES)
-        remote(rows_ref.at[g2], ebuf.at[g], e_send, e_recv, a, g2).start()
-        return c
-
-    lax.fori_loop(1, GRP, send_rows, 0)
+    land[a] = ids_ref[...]
+    for j in range(1, DP):
+        remote(ids_ref, land.at[a], i_send, i_recv, (a + j) % DP, g).start()
 
     half = pl.ds(pl.multiple_of(core * 64, 64), 64)
 
@@ -222,22 +193,95 @@
         wait_bytes(buf.at[l, :, half, :], f_recv.at[l, kind])
 
     send_weights(0, 0)
-    ebuf[g] = rows_ref[g]
+    send_weights(0, 1)
     kvs[...] = jnp.zeros_like(kvs)
+    wait_bytes(land.at[pl.ds(0, DP - 1)], i_recv)
+
+    number = DP * ALL
+    all_ref[...] = land[...]
+    along = jnp.concatenate([land[k] for k in range(DP)], axis=1).astype(F32)
+    line_of = lax.broadcasted_iota(jnp.int32, (1, number), 1).astype(F32)
+    line_id = along[0:1]
+    columns = []
+    for k in range(DP):
+        square = jnp.concatenate([along[:, k * ALL : (k + 1) * ALL]] * 16, axis=0)
+        columns.append(jnp.transpose(square)[:, 0:1])
+
+    def owner_of(ids):
+        return jnp.floor((ids + 0.5) * (1.0 / SHARD))
+
+    first_line = jnp.full((1, number), float(number), F32)
+    first_column = []
+    for k in range(DP):
+        same = columns[k] == line_id
+        up = lax.broadcasted_iota(jnp.int32, (ALL, number), 0).astype(F32) + float(k * ALL)
+        first_line = jnp.minimum(
+            first_line, jnp.min(jnp.where(same, up, float(number)), axis=0, keepdims=True)
+        )
+        first_column.append(jnp.min(jnp.where(same, line_of, float(number)), axis=1, keepdims=True))
+    is_first = first_line == line_of
+    line_owner = owner_of(line_id)
+    me = (a * GRP + g).astype(F32)
+
+    held = jnp.where(is_first & (line_owner == me), 1.0, 0.0)
+    earlier = lax.broadcasted_iota(jnp.int32, (number, number), 0) < lax.broadcasted_iota(
+        jnp.int32, (number, number), 1
+    )
+    earlier = jnp.where(earlier, 1.0, 0.0).astype(BF)
+    rank = jnp.dot(
+        jnp.broadcast_to(held, (8, number)).astype(BF), earlier, preferred_element_type=F32
+    )[0:1]
+    slot_no = lax.broadcasted_iota(jnp.int32, (SLOTS, number), 0).astype(F32)
+    local = jnp.sum(
+        jnp.where((held > 0.0) & (rank == slot_no), line_id - me * float(SHARD), 0.0),
+        axis=1,
+        keepdims=True,
+    )
+    entry = lax.broadcasted_iota(jnp.int32, (SLOTS, SHARD_WHOLE), 1).astype(F32)
+    take = jnp.where(entry == local, 1.0, 0.0).astype(BF)
+    tail = lax.broadcasted_iota(jnp.int32, (SLOTS, 16), 1).astype(F32) + float(SHARD_WHOLE)
+    take_tail = jnp.where(tail == local, 1.0, 0.0).astype(BF)
+    shard_copy.wait()
+    tail_v[...] = jnp.zeros_like(tail_v)
+    tail_v[0 : SHARD - SHARD_WHOLE, :] = shard_v[SHARD_WHOLE:SHARD, :]
+    rows = jnp.dot(take, shard_v[0:SHARD_WHOLE, :], preferred_element_type=F32)
+    rows = rows + jnp.dot(take_tail, tail_v[...], preferred_element_type=F32)
+    rows = rows.astype(BF)
+    for k in range(GRP):
+        rows_v[k] = rows[:, k * D : (k + 1) * D]
+
+    def send_rows(j, c):
+        g2 = ((z + j // SLICES) % PLANES) * SLICES + slice_at(j % SLICES)
+        remote(rows_v.at[g2], ebuf.at[g], e_send, e_recv, a, g2).start()
+        return c
+
+    lax.fori_loop(1, GRP, send_rows, 0)
+
+    ebuf[g] = rows_v[g]
+
+    most = jnp.zeros((ALL, 1), F32)
+    for k in range(DP):
+        owner = owner_of(columns[k])
+        before = is_first & (line_owner == owner) & (line_of < first_column[k])
+        slot = jnp.sum(jnp.where(before, 1.0, 0.0), axis=1, keepdims=True)
+        most = jnp.maximum(most, slot)
+        source = owner - (a * GRP).astype(F32)
+        ours = (source >= 0.0) & (source < float(GRP)) & (slot < float(SLOTS))
+        want = jnp.where(ours, source * float(SLOTS) + slot, -1.0)
+        place = lax.broadcasted_iota(jnp.int32, (ALL, GRP * SLOTS), 1).astype(F32)
+        chosen_v[k] = jnp.where(place == want, 1.0, 0.0).astype(BF)
+    most_ref[...] = jnp.broadcast_to(jnp.max(most, axis=0, keepdims=True), (8, ALL))
+
     wait_bytes(ebuf.at[pl.ds(0, GRP - 1)], e_recv)
     table = ebuf[...].reshape(GRP * SLOTS, D)
 
     def picked(a2):
-        want = idx_ref[pl.ds(pl.multiple_of(a2 * ALL, ALL), ALL), :]
-        place = lax.broadcasted_iota(jnp.int32, (ALL, GRP * SLOTS), 1)
-        chosen = jnp.where(place == want, 1.0, 0.0).astype(BF)
-        return jnp.dot(chosen, table, preferred_element_type=F32)
+        return jnp.dot(chosen_v[a2], table, preferred_element_type=F32)
 
     for j in range(1, DP):
         a2 = (a + j) % DP
         tbuf[j] = picked(a2).astype(BF)
         remote(tbuf.at[j], dbuf.at[j], d_send, d_recv, a2, g).start()
-    send_weights(0, 1)
     mine = picked(a) + extra_ref[...]
     wait_bytes(dbuf.at[pl.ds(1, DP - 1)], d_recv)
     for j in range(1, DP):
@@ -400,6 +444,7 @@
     for k in range(4):
         out_ref[:, k * D : (k + 1) * D] = final[k]
 
+    wait_bytes(land.at[pl.ds(0, DP - 1)], i_send)
     wait_bytes(ebuf.at[pl.ds(0, GRP - 1)], e_send)
     wait_bytes(dbuf.at[pl.ds(1, DP - 1)], d_send)
     for l in range(DECODER_LAYERS):
@@ -421,16 +466,19 @@
         wait_bytes(final, o_send)
 
 
-def decode(rows, idx, extra, gain, cosine, sine, lengths, wq, wo, cache):
+def decode(ids, extra, gain, cosine, sine, lengths, wq, wo, cache, embed):
     vmem = pl.BlockSpec(memory_space=pltpu.VMEM)
-    hbm = pl.BlockSpec(memory_space=pl.ANY)
+    hbm = pl.BlockSpec(memory_space=pltpu.HBM)
     layers = DECODER_LAYERS
     dma = pltpu.SemaphoreType.DMA
     return pl.pallas_call(
         main_kernel,
-        out_shape=jax.ShapeDtypeStruct((TOKENS, 512), BF),
+        out_shape=(
+            jax.ShapeDtypeStruct((TOKENS, 512), BF),
+            jax.ShapeDtypeStruct((DP, 8, ALL), jnp.int32),
+            jax.ShapeDtypeStruct((8, ALL), F32),
+        ),
         in_specs=[
-            vmem,
             vmem,
             vmem,
             vmem,
@@ -440,10 +488,16 @@
             hbm,
             hbm,
             hbm,
+            hbm,
         ],
-        out_specs=vmem,
+        out_specs=(vmem, vmem, vmem),
         scratch_shapes=[
             pltpu.VMEM((layers, REPLICA_ROWS, CACHE, 2 * D), BF),
+            pltpu.VMEM((SHARD, MODEL_WIDTH), BF),
+            pltpu.VMEM((DP, 8, ALL), jnp.int32),
+            pltpu.VMEM((16, MODEL_WIDTH), BF),
+            pltpu.VMEM((GRP, SLOTS, D), BF),
+            pltpu.VMEM((DP, ALL, GRP * SLOTS), BF),
             pltpu.VMEM((layers, SLICES, D, QKV), BF),
             pltpu.VMEM((layers, SLICES, D, 512), BF),
             pltpu.VMEM((GRP, SLOTS, D), BF),
@@ -482,12 +536,15 @@
             dma((layers,)),
             dma,
             dma,
+            dma,
+            dma,
+            dma,
         ],
         compiler_params=pltpu.CompilerParams(
-            collective_id=1, has_side_effects=True, vmem_limit_bytes=40 * 1024 * 1024
+            collective_id=1, has_side_effects=True, vmem_limit_bytes=48 * 1024 * 1024
         ),
         name="decode",
-    )(rows, idx, extra, gain, cosine, sine, lengths, wq, wo, cache)
+    )(ids, extra, gain, cosine, sine, lengths, wq, wo, cache, embed)
 
 
 def body(
@@ -506,36 +563,6 @@
     shard_rows = embed_table.shape[0]
     number = DP * ALL
 
-    ids = gather_ids(token_ids[0].transpose(0, 2, 1).reshape(ALL))[:, 0, :].reshape(number)
-    owner = ids // shard_rows
-    order = jnp.arange(number, dtype=jnp.int32)
-    same_id = ids[:, None] == ids[None, :]
-    first = jnp.min(jnp.where(same_id, order[None, :], number), axis=1)
-    is_first = first == order
-    before = is_first[None, :] & (owner[:, None] == owner[None, :]) & (order[None, :] < first[:, None])
-    slot = jnp.sum(before.astype(jnp.int32), axis=1)
-    holds = (
-        is_first[None, :]
-        & (owner[None, :] == me)
-        & (slot[None, :] == jnp.arange(SLOTS, dtype=jnp.int32)[:, None])
-    )
-    local = jnp.sum(jnp.where(holds, ids[None, :] - me * shard_rows, 0), axis=1)
-    rows = jnp.take(embed_table, local, axis=0, mode="clip")
-    rows = rows.reshape(SLOTS, GRP, D).transpose(1, 0, 2)
-    idx = jnp.where((owner // GRP == a) & (slot < SLOTS), (owner % GRP) * SLOTS + slot, -1)
-
-    def overflow(_):
-        late = (owner == me) & (slot >= SLOTS)
-        more = jnp.take(embed_table, jnp.where(late, ids - me * shard_rows, 0), axis=0, mode="clip")
-        more = jnp.where(late[:, None], more, jnp.zeros_like(more)).reshape(DP, ALL, GRP, D)
-        more = more.transpose(0, 2, 1, 3).reshape(DP * GRP, ALL, D)
-        more = lax.all_to_all(more, ("dp", "grp"), split_axis=0, concat_axis=0, tiled=True)
-        return jnp.sum(more.astype(F32), axis=0)
-
-    extra = lax.cond(
-        jnp.max(slot) >= SLOTS, overflow, lambda _: jnp.zeros((ALL, D), F32), jnp.int32(0)
-    )
-
     lengths = lax.dynamic_index_in_dim(cache_len[0], z, 0, keepdims=False)
     starts = lax.dynamic_index_in_dim(start_pos[0], z, 0, keepdims=False)
     position = (starts[None, :] + jnp.arange(DECODE_STEPS, dtype=jnp.int32)[:, None]).reshape(TOKENS)
@@ -547,18 +574,42 @@
     sine = jnp.concatenate([-sine, sine], axis=1)
     gain = lax.dynamic_slice_in_dim(norm_gain, g * D, D, 1).reshape(DECODER_LAYERS, 1, D)
 
-    out = decode(
-        rows,
-        idx.reshape(number, 1),
-        extra,
-        gain,
-        cosine,
-        sine,
-        lengths,
-        query_key_value_weight,
-        output_weight,
-        key_value_cache.reshape(DECODER_LAYERS, REPLICA_ROWS, CACHE, 2 * D),
-    )
+    def run(extra):
+        return decode(
+            ids,
+            extra,
+            gain,
+            cosine,
+            sine,
+            lengths,
+            query_key_value_weight,
+            output_weight,
+            key_value_cache.reshape(DECODER_LAYERS, REPLICA_ROWS, CACHE, 2 * D),
+            embed_table,
+        )
+
+    ids = jnp.broadcast_to(token_ids[0].transpose(0, 2, 1).reshape(1, ALL), (8, ALL))
+    out, everyone, most = run(jnp.zeros((ALL, D), F32))
+
+    def again(_):
+        flat = everyone[:, 0, :].reshape(DP * ALL)
+        owner = flat // shard_rows
+        order = jnp.arange(DP * ALL, dtype=jnp.int32)
+        first = jnp.min(jnp.where(flat[:, None] == flat[None, :], order[None, :], DP * ALL), axis=1)
+        before = (
+            (first == order)[None, :]
+            & (owner[:, None] == owner[None, :])
+            & (order[None, :] < first[:, None])
+        )
+        slot = jnp.sum(before.astype(jnp.int32), axis=1)
+        late = (owner == me) & (slot >= SLOTS)
+        more = jnp.take(embed_table, jnp.where(late, flat - me * shard_rows, 0), axis=0, mode="clip")
+        more = jnp.where(late[:, None], more, jnp.zeros_like(more)).reshape(DP, ALL, GRP, D)
+        more = more.transpose(0, 2, 1, 3).reshape(DP * GRP, ALL, D)
+        more = lax.all_to_all(more, ("dp", "grp"), split_axis=0, concat_axis=0, tiled=True)
+        return run(jnp.sum(more.astype(F32), axis=0))[0]
+
+    out = lax.cond(most[0, 0] >= SLOTS, again, lambda _: out, jnp.int32(0))
     return out.reshape(DECODE_STEPS, REPLICA_ROWS, 512).transpose(1, 0, 2)[:, None]
 
 

time: 118 us -> 96 us (0.81)
  local copies, waits for them, and re-layouts: 15.5 us -> 2.84 us
  Pallas kernels: 96.5 us -> 91.7 us
  other arithmetic: 4.72 us -> 0.31 us
    gather x1 -> x0, local copies, waits for them, and re-layouts: 5.15 us -> none  [body(): rows = jnp.take(embed_table, local, axis=0, mode='clip')]
    unnamed x8 -> x4, local copies, waits for them, and re-layouts: 4.98 us -> 0.01 us
    pallas_call x2 -> x1, Pallas kernels: 96.5 us -> 91.7 us  [decode(): pl.pallas_call(main_kernel, out_shape=(jax.ShapeDtypeStruct((TOKENS, 512)...]
    select_n x1 -> x0, other arithmetic: 1.38 us -> none  [body(): jnp.where((owner // GRP == a) & (slot < SLOTS), owner % GRP * SLOTS + slo...]
where the time goes in v3:
time: 96 us; the launch traced here: 95.8 us
  Pallas kernels  91.7 us (96%)
  local copies, waits for them, and re-layouts  2.84 us (3%)
    pallas_call x1, Pallas kernels, decode(): pl.pallas_call(main_kernel, out_shape=(jax.ShapeDtypeStruct((TOKENS, 512)...  91.7 us

profile of v3, /device:TPU:8, one launch (start us, length us, event | category | flops | bytes accessed | tf_op | source)
XLA Modules:
  0.0 95.8 jit_solution(15610102477240568764)
XLA Ops:
  0.0 0.0 copy-start
  0.0 0.8 broadcast_in_dim.50
  0.8 0.0 copy-done
  0.8 0.7 fusion.6
  1.6 0.1 convert_element_type.23
  1.6 0.1 fusion.5
  1.8 0.1 pad_maximum_fusion.1.sin_ref
  1.9 0.1 pad_maximum_fusion.cos_ref
  2.0 0.0 copy-start.1
  2.0 91.7 %decode.3 = (bf16[32,512]{1,0:T(8,128)(2,1)S(1)}, s32[4,8,128]{2,1,0:T(8,128)S(1)}, f32[8,128]{1,0:T(8,128)S(1)}) custom-call(s32[8,128]{1,0:T(8,128)S(1)} %broadcast_in_dim.51.ids_ref, f32[128,128]{1,0:T(8,128)S(1)} %broadcast_in_dim.52.extra_ref, f32[2,1,128]{2,1,0:T(1,128)S(1)} %bitcast.53, f32[32,128]{1,0:T(8,128)S(1)} %pad_maximum_fusion.cos_ref, ...), custom_call_target="tpu_custom_call" | custom-call | tf_op jit(solution)/shard_map/decode/pallas_call | solution.py:474
  93.7 0.6 slice.6
  94.9 0.0 copy-done.1
  95.0 0.2 conditional.1
  95.2 0.6 copy.18
  (5 shorter events, 0.0 us)
Async XLA Ops:
  0.0 0.8 copy-start
  2.0 93.0 %copy-start.1 = (bf16[2,128,6144]{2,1,0:T(8,128)(2,1)S(1)}, bf16[2,128,6144]{2,1,0:T(8,128)(2,1)}, u32[]{:S(2)}) copy-start(bf16[2,128,6144]{2,1,0:T(8,128)(2,1)} %wq_ref.1) | copy-start | bytes 9437188

commit v4 on v3

--- a/solution.py
+++ b/solution.py
@@ -131,15 +131,24 @@
     lax.fori_loop(1, GRP, greet, 0)
     for j in range(1, DP):
         pl.semaphore_signal(barrier, inc=1, device_id=((a + j) % DP, g), device_id_type=MESH)
-    pl.semaphore_wait(barrier, GRP - 1 + DP - 1)
+
+    def greet_across(k, c):
+        g2 = z * SLICES + (1 - y) * 4 + k
+        pl.semaphore_signal(barrier, inc=1, device_id=((a + 2) % DP, g2), device_id_type=MESH)
+        return c
+
+    lax.fori_loop(0, 4, greet_across, 0)
+    pl.semaphore_wait(barrier, GRP - 1 + DP - 1 + 4)
 
     land[a] = ids_ref[...]
     for j in range(1, DP):
         remote(ids_ref, land.at[a], i_send, i_recv, (a + j) % DP, g).start()
 
     half = pl.ds(pl.multiple_of(core * 64, 64), 64)
-
-    def qkv_pieces(l, t2):
+    halves = [pl.ds(pl.multiple_of(core * 64 + k * 32, 32), 32) for k in range(2)]
+    across = (a + 2) % DP
+
+    def qkv_pieces(l, t2, half):
         return (
             (
                 wq_ref.at[l, half, pl.ds(pl.multiple_of(t2 * 512, 512), 512)],
@@ -155,7 +164,7 @@
             ),
         )
 
-    def out_pieces(l, t2):
+    def out_pieces(l, t2, half):
         return (
             (
                 wo_ref.at[l, half, pl.ds(pl.multiple_of(t2 * 512, 512), 512)],
@@ -166,14 +175,23 @@
     def send_weights(l, kind):
         pieces = (qkv_pieces, out_pieces)[kind]
 
+        def send(j, rows, a2):
+            t2 = slice_at(j)
+            for src, dst in pieces(l, t2, rows):
+                remote(src, dst, w_send.at[l, kind], w_recv.at[l, kind], a2, z * SLICES + t2).start()
+
         def one(j, c):
-            t2 = slice_at(j)
-            for src, dst in pieces(l, t2):
-                remote(src, dst, w_send.at[l, kind], w_recv.at[l, kind], a, z * SLICES + t2).start()
+            send(j, half, a)
             return c
 
-        lax.fori_loop(1, SLICES, one, 0)
-        for src, dst in pieces(l, t):
+        def both(j, c):
+            send(j, halves[0], a)
+            send(j, halves[1], across)
+            return c
+
+        lax.fori_loop(4, SLICES, both, 0)
+        lax.fori_loop(1, 4, one, 0)
+        for src, dst in pieces(l, t, half):
             pltpu.make_async_copy(src, dst, w_recv.at[l, kind]).start()
 
     def forward_weights(l, kind):
@@ -193,7 +211,6 @@
         wait_bytes(buf.at[l, :, half, :], f_recv.at[l, kind])
 
     send_weights(0, 0)
-    send_weights(0, 1)
     kvs[...] = jnp.zeros_like(kvs)
     wait_bytes(land.at[pl.ds(0, DP - 1)], i_recv)
 
@@ -256,6 +273,7 @@
         return c
 
     lax.fori_loop(1, GRP, send_rows, 0)
+    send_weights(0, 1)
 
     ebuf[g] = rows_v[g]
 
@@ -319,6 +337,10 @@
         forward_weights(l, 0)
         wait_bytes(p1r.at[l, pl.ds(0, SLICES - 1)], p1_recv.at[l])
         await_weights(l, 0)
+        if l + 1 < DECODER_LAYERS:
+            send_weights(l + 1, 0)
+        if l + 1 < DECODER_LAYERS:
+            send_weights(l + 1, 1)
 
         left = jnp.concatenate([p1r[l, j, 0:ALL, :] for j in range(SLICES)], axis=1)
         sums = jnp.zeros((8, ALL), F32)
@@ -342,8 +364,6 @@
             ).start()
         forward_weights(l, 1)
         wait_bytes(p2r.at[l, pl.ds(1, PLANES - 1)], p2_recv.at[l])
-        if l + 1 < DECODER_LAYERS:
-            send_weights(l + 1, 0)
         total = p2s[l, z].astype(F32)
         for j in range(1, PLANES):
             total = total + p2r[l, j].astype(F32)
@@ -398,8 +418,6 @@
         p3r[l, z] = p3s[l]
         await_weights(l, 1)
         wait_bytes(p3r.at[l, pl.ds(0, PLANES - 1)], p3_recv.at[l])
-        if l + 1 < DECODER_LAYERS:
-            send_weights(l + 1, 1)
         left = jnp.concatenate(
             [
                 jnp.concatenate(

time: 96 us -> 86.4 us (0.900)
  Pallas kernels: 91.7 us -> 82.1 us
    pallas_call x1, Pallas kernels: 91.7 us -> 82.1 us  [decode(): pl.pallas_call(main_kernel, out_shape=(jax.ShapeDtypeStruct((TOKENS, 512)...]
where the time goes in v4:
time: 86.4 us; the launch traced here: 86.2 us
  Pallas kernels  82.1 us (95%)
  local copies, waits for them, and re-layouts  2.84 us (3%)
    pallas_call x1, Pallas kernels, decode(): pl.pallas_call(main_kernel, out_shape=(jax.ShapeDtypeStruct((TOKENS, 512)...  82.1 us

profile of v4, /device:TPU:8, one launch (start us, length us, event | category | flops | bytes accessed | tf_op | source)
XLA Modules:
  0.0 86.2 jit_solution(676697700769284038)
XLA Ops:
  0.0 0.0 copy-start
  0.0 0.8 broadcast_in_dim.50
  0.8 0.0 copy-done
  0.8 0.7 fusion.6
  1.6 0.1 convert_element_type.23
  1.6 0.1 fusion.5
  1.8 0.1 pad_maximum_fusion.1.sin_ref
  1.9 0.1 pad_maximum_fusion.cos_ref
  2.0 0.0 copy-start.1
  2.0 82.1 %decode.3 = (bf16[32,512]{1,0:T(8,128)(2,1)S(1)}, s32[4,8,128]{2,1,0:T(8,128)S(1)}, f32[8,128]{1,0:T(8,128)S(1)}) custom-call(s32[8,128]{1,0:T(8,128)S(1)} %broadcast_in_dim.51.ids_ref, f32[128,128]{1,0:T(8,128)S(1)} %broadcast_in_dim.52.extra_ref, f32[2,1,128]{2,1,0:T(1,128)S(1)} %bitcast.53, f32[32,128]{1,0:T(8,128)S(1)} %pad_maximum_fusion.cos_ref, ...), custom_call_target="tpu_custom_call" | custom-call | tf_op jit(solution)/shard_map/decode/pallas_call | solution.py:492
  84.1 0.6 slice.6
  85.4 0.0 copy-done.1
  85.4 0.2 conditional.1
  85.6 0.6 copy.18
  (5 shorter events, 0.0 us)
Async XLA Ops:
  0.0 0.8 copy-start
  2.0 83.4 %copy-start.1 = (bf16[2,128,6144]{2,1,0:T(8,128)(2,1)S(1)}, bf16[2,128,6144]{2,1,0:T(8,128)(2,1)}, u32[]{:S(2)}) copy-start(bf16[2,128,6144]{2,1,0:T(8,128)(2,1)} %wq_ref.1) | copy-start | bytes 9437188

commit v5 on v4

--- a/solution.py
+++ b/solution.py
@@ -21,6 +21,7 @@
 PLANES = 4
 SLICES = 8
 GRP = PLANES * SLICES
+FAR_FIRST = (6, 5, 7, 2, 4, 1, 3)
 TOKENS = REPLICA_ROWS * DECODE_STEPS
 ALL = PLANES * TOKENS
 D = 128
@@ -288,7 +289,7 @@
         want = jnp.where(ours, source * float(SLOTS) + slot, -1.0)
         place = lax.broadcasted_iota(jnp.int32, (ALL, GRP * SLOTS), 1).astype(F32)
         chosen_v[k] = jnp.where(place == want, 1.0, 0.0).astype(BF)
-    most_ref[...] = jnp.broadcast_to(jnp.max(most, axis=0, keepdims=True), (8, ALL))
+    most_ref[0] = jnp.max(most).astype(jnp.int32)
 
     wait_bytes(ebuf.at[pl.ds(0, GRP - 1)], e_recv)
     table = ebuf[...].reshape(GRP * SLOTS, D)
@@ -332,7 +333,8 @@
             ).start()
             return c
 
-        lax.fori_loop(1, SLICES, send_stream, 0)
+        for j in FAR_FIRST:
+            send_stream(j, 0)
         p1r[l, t] = p1s[l]
         forward_weights(l, 0)
         wait_bytes(p1r.at[l, pl.ds(0, SLICES - 1)], p1_recv.at[l])
@@ -357,7 +359,7 @@
                     r * TOKENS : (r + 1) * TOKENS, c * D : (c + 1) * D
                 ]
             p2s[l, r, 192:208, :] = sums
-        for j in range(1, PLANES):
+        for j in (2, 1, 3):
             z2 = (z + j) % PLANES
             remote(
                 p2s.at[l, z2], p2r.at[l, j], p2_send.at[l], p2_recv.at[l], a, z2 * SLICES + t
@@ -410,7 +412,7 @@
             atts[pl.ds(b, 16, stride=8), :] = value / whole
 
         p3s[l] = atts[...].astype(BF)
-        for j in range(1, PLANES):
+        for j in (2, 1, 3):
             z2 = (z + j) % PLANES
             remote(
                 p3s.at[l], p3r.at[l, z], p3_send.at[l], p3_recv.at[l], a, z2 * SLICES + t
@@ -431,7 +433,7 @@
         def partial(t2):
             return lax.dot_general(left, wox[l, t2], contract, preferred_element_type=F32)
 
-        for j in range(1, SLICES):
+        for j in FAR_FIRST:
             t2 = slice_at(j)
             p4s[l, j] = partial(t2).astype(BF)
             remote(
@@ -494,7 +496,7 @@
         out_shape=(
             jax.ShapeDtypeStruct((TOKENS, 512), BF),
             jax.ShapeDtypeStruct((DP, 8, ALL), jnp.int32),
-            jax.ShapeDtypeStruct((8, ALL), F32),
+            jax.ShapeDtypeStruct((1,), jnp.int32),
         ),
         in_specs=[
             vmem,
@@ -508,7 +510,7 @@
             hbm,
             hbm,
         ],
-        out_specs=(vmem, vmem, vmem),
+        out_specs=(vmem, vmem, pl.BlockSpec(memory_space=pltpu.SMEM)),
         scratch_shapes=[
             pltpu.VMEM((layers, REPLICA_ROWS, CACHE, 2 * D), BF),
             pltpu.VMEM((SHARD, MODEL_WIDTH), BF),
@@ -627,7 +629,7 @@
         more = lax.all_to_all(more, ("dp", "grp"), split_axis=0, concat_axis=0, tiled=True)
         return run(jnp.sum(more.astype(F32), axis=0))[0]
 
-    out = lax.cond(most[0, 0] >= SLOTS, again, lambda _: out, jnp.int32(0))
+    out = lax.cond(most[0] >= SLOTS, again, lambda _: out, jnp.int32(0))
     return out.reshape(DECODE_STEPS, REPLICA_ROWS, 512).transpose(1, 0, 2)[:, None]
 
 

time: 86.4 us -> 83.8 us (0.970)
  Pallas kernels: 82.1 us -> 80.1 us
    pallas_call x1, Pallas kernels: 82.1 us -> 80.1 us  [decode(): pl.pallas_call(main_kernel, out_shape=(jax.ShapeDtypeStruct((TOKENS, 512)...]
where the time goes in v5:
time: 83.8 us; the launch traced here: 83.6 us
  Pallas kernels  80.1 us (96%)
  local copies, waits for them, and re-layouts  2.25 us (3%)
    pallas_call x1, Pallas kernels, decode(): pl.pallas_call(main_kernel, out_shape=(jax.ShapeDtypeStruct((TOKENS, 512)...  80.1 us

profile of v5, /device:TPU:8, one launch (start us, length us, event | category | flops | bytes accessed | tf_op | source)
XLA Modules:
  0.0 83.6 jit_solution(2646636011447321253)
XLA Ops:
  0.0 0.0 copy-start
  0.0 0.8 broadcast_in_dim.50
  0.8 0.0 copy-done
  0.8 0.7 fusion.6
  1.6 0.1 convert_element_type.23
  1.6 0.1 fusion.5
  1.8 0.1 pad_maximum_fusion.1.sin_ref
  1.9 0.1 pad_maximum_fusion.cos_ref
  2.0 0.0 copy-start.1
  2.0 80.1 %decode.3 = (bf16[32,512]{1,0:T(8,128)(2,1)S(1)}, s32[4,8,128]{2,1,0:T(8,128)S(1)}, s32[1]{0:T(128)}) custom-call(s32[8,128]{1,0:T(8,128)S(1)} %broadcast_in_dim.51.ids_ref, f32[128,128]{1,0:T(8,128)S(1)} %broadcast_in_dim.52.extra_ref, f32[2,1,128]{2,1,0:T(1,128)S(1)} %bitcast.53, f32[32,128]{1,0:T(8,128)S(1)} %pad_maximum_fusion.cos_ref, ...), custom_call_target="tpu_custom_call" | custom-call | tf_op jit(solution)/shard_map/decode/pallas_call | solution.py:494
  82.8 0.0 copy-done.1
  82.8 0.2 conditional.1
  83.0 0.6 copy.18
  (5 shorter events, 0.0 us)
Async XLA Ops:
  0.0 0.8 copy-start
  2.0 80.8 %copy-start.1 = (bf16[2,128,6144]{2,1,0:T(8,128)(2,1)S(1)}, bf16[2,128,6144]{2,1,0:T(8,128)(2,1)}, u32[]{:S(2)}) copy-start(bf16[2,128,6144]{2,1,0:T(8,128)(2,1)} %wq_ref.1) | copy-start | bytes 9437188

commit v6 on v5

--- a/solution.py
+++ b/solution.py
@@ -190,8 +190,8 @@
             send(j, halves[1], across)
             return c
 
-        lax.fori_loop(4, SLICES, both, 0)
-        lax.fori_loop(1, 4, one, 0)
+        for j in FAR_FIRST:
+            (both if j >= 4 else one)(j, 0)
         for src, dst in pieces(l, t, half):
             pltpu.make_async_copy(src, dst, w_recv.at[l, kind]).start()
 
@@ -273,7 +273,10 @@
         remote(rows_v.at[g2], ebuf.at[g], e_send, e_recv, a, g2).start()
         return c
 
-    lax.fori_loop(1, GRP, send_rows, 0)
+    for j in FAR_FIRST + (0,):
+        for k in (2, 1, 3, 0):
+            if j + k > 0:
+                send_rows(k * SLICES + j, 0)
     send_weights(0, 1)
 
     ebuf[g] = rows_v[g]

time: 83.8 us -> 82.5 us (0.984)
  Pallas kernels: 80.1 us -> 78.8 us
    pallas_call x1, Pallas kernels: 80.1 us -> 78.8 us  [decode(): pl.pallas_call(main_kernel, out_shape=(jax.ShapeDtypeStruct((TOKENS, 512)...]
where the time goes in v6:
time: 82.5 us; the launch traced here: 82.3 us
  Pallas kernels  78.8 us (96%)
  local copies, waits for them, and re-layouts  2.25 us (3%)
    pallas_call x1, Pallas kernels, decode(): pl.pallas_call(main_kernel, out_shape=(jax.ShapeDtypeStruct((TOKENS, 512)...  78.8 us

profile of v6, /device:TPU:8, one launch (start us, length us, event | category | flops | bytes accessed | tf_op | source)
XLA Modules:
  0.0 82.3 jit_solution(14067702218188628993)
XLA Ops:
  0.0 0.0 copy-start
  0.0 0.8 broadcast_in_dim.50
  0.8 0.0 copy-done
  0.8 0.7 fusion.6
  1.6 0.1 convert_element_type.23
  1.6 0.1 fusion.5
  1.8 0.1 pad_maximum_fusion.1.sin_ref
  1.9 0.1 pad_maximum_fusion.cos_ref
  2.0 0.0 copy-start.1
  2.0 78.8 %decode.3 = (bf16[32,512]{1,0:T(8,128)(2,1)S(1)}, s32[4,8,128]{2,1,0:T(8,128)S(1)}, s32[1]{0:T(128)}) custom-call(s32[8,128]{1,0:T(8,128)S(1)} %broadcast_in_dim.51.ids_ref, f32[128,128]{1,0:T(8,128)S(1)} %broadcast_in_dim.52.extra_ref, f32[2,1,128]{2,1,0:T(1,128)S(1)} %bitcast.53, f32[32,128]{1,0:T(8,128)S(1)} %pad_maximum_fusion.cos_ref, ...), custom_call_target="tpu_custom_call" | custom-call | tf_op jit(solution)/shard_map/decode/pallas_call | solution.py:497
  81.4 0.0 copy-done.1
  81.5 0.2 conditional.1
  81.7 0.6 copy.18
  (5 shorter events, 0.0 us)
Async XLA Ops:
  0.0 0.8 copy-start
  2.0 79.5 %copy-start.1 = (bf16[2,128,6144]{2,1,0:T(8,128)(2,1)S(1)}, bf16[2,128,6144]{2,1,0:T(8,128)(2,1)}, u32[]{:S(2)}) copy-start(bf16[2,128,6144]{2,1,0:T(8,128)(2,1)} %wq_ref.1) | copy-start | bytes 9437188
